TPU v7x, 256 devices: a whole 4x4x8 slice. The times are simulated.
256 devices in a mesh: ctx: 16 (over y_hi, z), head: 16 (over y_lo, x, core).
Axes of the slice: x: 4, y: 4 (y_hi: 2, y_lo: 2; y = y_hi * 2 + y_lo), z: 8, core: 2. Of those that a mesh axis runs over, the one named last changes fastest.
Arguments:
- key_rows: bfloat16 [32768, 4096], P('ctx', 'head'), may hold values from -4 to 4
- query_rows: bfloat16 [32768, 4096], P('ctx', 'head'), may hold values from -4 to 4
- row_lse: bfloat16 [32, 32768], P('head', 'ctx'), may hold values from 10.5 to 12.5
- query_offsets: int32 [32768], P('ctx'), may hold values from 0 to 2047
Outputs:
- key_mass: float32 [32768], P(('ctx', 'head'))
All inputs are finite; a program needn't handle non-finite values.
Results may differ from a plain program's by a relative error of at most 0.0003.
Values may be sent and summed in bfloat16 or wider, within the bound.
No kernel may reach another device: no remote copies, remote signals or barrier semaphores. Data moves between devices by JAX's collectives and lax.ppermute only.
A program may use at most 64 MiB of HBM per device.

v0:
```python
import jax
import jax.numpy as jnp
from jax import lax
from jax.sharding import PartitionSpec as P

HD = 128


def from_behind(value, axis, steps):
    count = lax.axis_size(axis)
    leading, last = (max(0, -steps), min(count, count - steps))
    return lax.ppermute(value, axis, [(source, source + steps) for source in range(leading, last)])


def block_mass(key_heads, query_heads, lse_rows, offsets, own_block, is_live):
    softmax_scale = 1.0 / HD**0.5
    key_count = key_heads.shape[0]
    row_count = query_heads.shape[0]
    block_size = min(512, row_count)
    key_index = jnp.arange(key_count, dtype=jnp.int32)
    running = jnp.zeros((key_count,), jnp.float32)
    for first_row in range(0, row_count, block_size):
        scores = (
            jnp.einsum(
                "qhd,khd->hqk",
                query_heads[first_row : first_row + block_size],
                key_heads,
                preferred_element_type=jnp.float32,
            )
            * softmax_scale
        )
        weights = jnp.exp(
            scores - lse_rows[:, first_row : first_row + block_size, None].astype(jnp.float32)
        )
        if own_block:
            allowed = key_index[None, :] <= offsets[first_row : first_row + block_size, None]
            weights = jnp.where(allowed[None], weights, 0.0)
        running = running + jnp.sum(weights, axis=(0, 1))
    return running * is_live


def on_device(key_rows, query_rows, row_lse, query_offsets):
    heads_local = key_rows.shape[1] // HD
    key_heads = key_rows.reshape(key_rows.shape[0], heads_local, HD)
    own_index = lax.axis_index("ctx")
    cycle_size = lax.axis_size("ctx")
    query_heads = query_rows.reshape(query_rows.shape[0], heads_local, HD)
    partials = [block_mass(key_heads, query_heads, row_lse, query_offsets, True, jnp.float32(1.0))]
    travelling = (query_rows, row_lse)
    for distance in range(1, 4):
        travelling = from_behind((travelling[0], travelling[1]), "ctx", -1)
        is_live = (own_index + distance < cycle_size).astype(jnp.float32)
        arrived_heads = travelling[0].reshape(travelling[0].shape[0], heads_local, HD)
        partials.append(
            block_mass(key_heads, arrived_heads, travelling[1], query_offsets, False, is_live)
        )
    running = partials[0] + partials[1] + partials[2] + partials[3]
    return lax.psum_scatter(running, "head", scatter_dimension=0, tiled=True)


def solution(mesh):
    in_specs = (P("ctx", "head"), P("ctx", "head"), P("head", "ctx"), P("ctx"))
    out_specs = P(("ctx", "head"))
    return jax.shard_map(
        on_device, mesh=mesh, in_specs=in_specs, out_specs=out_specs, check_vma=False
    )
```

profile of v0, /device:TPU:17, one launch (start us, length us, event | category | flops | bytes accessed | tf_op | source)
XLA Modules:
  0.0 141.8 jit_solution(2466159581967867167)
XLA Ops:
  0.0 7.4 %collective-permute-start.1 = (bf16[2,2048]{1,0:T(2,128)(2,1)}, bf16[2,2048]{1,0:T(2,128)(2,1)S(1)}, u32[]{:S(2)}, u32[]{:S(2)}) collective-permute-start(bf16[2,2048]{1,0:T(2,128)(2,1)} %param.6), channel_id=1, source_target_pairs={{16,0},{32,16},{48,32},{64,48},{80,64},{96,80},{112,96},{128,112},... | collective-permute-start | bytes 24584 | tf_op jit(solution)/shard_map/ppermute | solution.py:12
  8.9 2.6 %collective-permute-start = (bf16[2048,256]{0,1:T(8,128)(2,1)S(1)}, bf16[2048,256]{0,1:T(8,128)(2,1)S(1)}, u32[]{:S(2)}, u32[]{:S(2)}) collective-permute-start(bf16[2048,256]{0,1:T(8,128)(2,1)S(1)} %copy.58), channel_id=1, source_target_pairs={{16,0},{32,16},{48,32},{64,48},{80,64},{96,80},{112,96},{128,112},... | collective-permute-start | bytes 3145736 | tf_op jit(solution)/shard_map/ppermute | solution.py:12
  15.4 3.2 %select_reduce_fusion.3 = f32[2048]{0:T(1024)S(1)} fusion(bf16[512,2,128]{0,2,1:T(8,128)(2,1)S(1)} %bitcast.142, f32[2,512]{1,0:T(2,128)S(1)} %get-tuple-element.27, pred[512,2048]{1,0:T(8,128)(4,1)S(1)} %get-tuple-element.44, bf16[2048,256]{1,0:T(8,128)(2,1)S(1)} %copy-done), kind=kOutput, calls=%fused_computation.15 | convolution fusion | flops 545257472 | bytes 2371584 | tf_op jit(solution)/shard_map/qhd,khd->hqk/dot_general | solution.py:24
  18.6 3.2 %select_reduce_fusion.2 = f32[2048]{0:T(1024)S(1)} fusion(bf16[512,2,128]{0,2,1:T(8,128)(2,1)S(1)} %bitcast.141, f32[2,512]{1,0:T(2,128)S(1)} %get-tuple-element.25, pred[512,2048]{1,0:T(8,128)(4,1)S(1)} %get-tuple-element.43, bf16[2048,256]{1,0:T(8,128)(2,1)S(1)} %copy-done), kind=kOutput, calls=%fused_computation.14 | convolution fusion | flops 545257472 | bytes 2371584 | tf_op jit(solution)/shard_map/qhd,khd->hqk/dot_general | solution.py:24
  21.8 3.2 %select_reduce_fusion.1 = f32[2048]{0:T(1024)S(1)} fusion(bf16[512,2,128]{0,2,1:T(8,128)(2,1)S(1)} %bitcast.140, f32[2,512]{1,0:T(2,128)S(1)} %get-tuple-element.26, pred[512,2048]{1,0:T(8,128)(4,1)S(1)} %get-tuple-element.42, bf16[2048,256]{1,0:T(8,128)(2,1)S(1)} %copy-done), kind=kOutput, calls=%fused_computation.13 | convolution fusion | flops 545257472 | bytes 2371584 | tf_op jit(solution)/shard_map/qhd,khd->hqk/dot_general | solution.py:24
  25.1 3.2 %select_reduce_fusion = f32[2048]{0:T(1024)S(1)} fusion(bf16[512,2,128]{0,2,1:T(8,128)(2,1)S(1)} %bitcast.139, f32[2,512]{1,0:T(2,128)S(1)} %get-tuple-element.28, pred[512,2048]{1,0:T(8,128)(4,1)S(1)} %get-tuple-element.41, bf16[2048,256]{1,0:T(8,128)(2,1)S(1)} %copy-done), kind=kOutput, calls=%fused_computation.12 | convolution fusion | flops 545257472 | bytes 2371584 | tf_op jit(solution)/shard_map/qhd,khd->hqk/dot_general | solution.py:24
  29.6 2.6 %collective-permute-start.3 = (bf16[2,2048]{1,0:T(2,128)(2,1)S(1)}, bf16[2,2048]{1,0:T(2,128)(2,1)S(1)}, u32[]{:S(2)}, u32[]{:S(2)}) collective-permute-start(bf16[2,2048]{1,0:T(2,128)(2,1)S(1)} %collective-permute-done.1), channel_id=1, source_target_pairs={{16,0},{32,16},{48,32},{64,48},{80,64},{96,80},{112,96},{128,112},... | collective-permute-start | bytes 24584 | tf_op jit(solution)/shard_map/ppermute | solution.py:12
  32.2 2.4 %collective-permute-done.3 = bf16[2,2048]{1,0:T(2,128)(2,1)S(1)} collective-permute-done((bf16[2,2048]{1,0:T(2,128)(2,1)S(1)}, bf16[2,2048]{1,0:T(2,128)(2,1)S(1)}, u32[]{:S(2)}, u32[]{:S(2)}) %collective-permute-start.3) | collective-permute-done | bytes 8224 | tf_op jit(solution)/shard_map/ppermute | solution.py:12
  34.7 6.2 %collective-permute-start.5 = (bf16[2,2048]{1,0:T(2,128)(2,1)S(1)}, bf16[2,2048]{1,0:T(2,128)(2,1)S(1)}, u32[]{:S(2)}, u32[]{:S(2)}) collective-permute-start(bf16[2,2048]{1,0:T(2,128)(2,1)S(1)} %collective-permute-done.3), channel_id=1, source_target_pairs={{16,0},{32,16},{48,32},{64,48},{80,64},{96,80},{112,96},{128,112},... | collective-permute-start | bytes 24584 | tf_op jit(solution)/shard_map/ppermute | solution.py:12
  41.8 2.3 %exponential_reduce_fusion.10 = f32[2048]{0:T(1024)S(1)} fusion(f32[2,512]{1,0:T(2,128)S(1)} %get-tuple-element.29, bf16[512,2,128]{0,2,1:T(8,128)(2,1)S(1)} %bitcast.153, bf16[2048,256]{1,0:T(8,128)(2,1)S(1)} %copy-done), kind=kOutput, calls=%fused_computation.10 | convolution fusion | flops 543160320 | bytes 1323008 | tf_op jit(solution)/shard_map/qhd,khd->hqk/dot_general | solution.py:24
  44.1 7.4 %collective-permute-start.2 = (bf16[2048,256]{0,1:T(8,128)(2,1)S(1)}, bf16[2048,256]{0,1:T(8,128)(2,1)S(1)}, u32[]{:S(2)}, u32[]{:S(2)}) collective-permute-start(bf16[2048,256]{0,1:T(8,128)(2,1)S(1)} %collective-permute-done), channel_id=1, source_target_pairs={{16,0},{32,16},{48,32},{64,48},{80,64},{96,80},{112,96},{128,112},... | collective-permute-start | bytes 3145736 | tf_op jit(solution)/shard_map/ppermute | solution.py:12
  51.5 2.3 %exponential_reduce_fusion.8 = f32[2048]{0:T(1024)S(1)} fusion(f32[2,512]{1,0:T(2,128)S(1)} %get-tuple-element.30, bf16[512,2,128]{0,2,1:T(8,128)(2,1)S(1)} %bitcast.148, bf16[2048,256]{1,0:T(8,128)(2,1)S(1)} %copy-done), kind=kOutput, calls=%fused_computation.8 | convolution fusion | flops 543160320 | bytes 1323008 | tf_op jit(solution)/shard_map/qhd,khd->hqk/dot_general | solution.py:24
  53.8 2.3 %exponential_reduce_fusion.9 = f32[2048]{0:T(1024)S(1)} fusion(f32[2,512]{1,0:T(2,128)S(1)} %get-tuple-element.31, bf16[512,2,128]{0,2,1:T(8,128)(2,1)S(1)} %bitcast.145, bf16[2048,256]{1,0:T(8,128)(2,1)S(1)} %copy-done), kind=kOutput, calls=%fused_computation.9 | convolution fusion | flops 543160320 | bytes 1323008 | tf_op jit(solution)/shard_map/qhd,khd->hqk/dot_general | solution.py:24
  56.1 2.3 %exponential_reduce_fusion.11 = f32[2048]{0:T(1024)S(1)} fusion(f32[2,512]{1,0:T(2,128)S(1)} %get-tuple-element.32, bf16[512,2,128]{0,2,1:T(8,128)(2,1)S(1)} %bitcast.143, bf16[2048,256]{1,0:T(8,128)(2,1)S(1)} %copy-done), kind=kOutput, calls=%fused_computation.11 | convolution fusion | flops 543160320 | bytes 1323008 | tf_op jit(solution)/shard_map/qhd,khd->hqk/dot_general | solution.py:24
  58.4 12.3 %collective-permute-done.2 = bf16[2048,256]{0,1:T(8,128)(2,1)S(1)} collective-permute-done((bf16[2048,256]{0,1:T(8,128)(2,1)S(1)}, bf16[2048,256]{0,1:T(8,128)(2,1)S(1)}, u32[]{:S(2)}, u32[]{:S(2)}) %collective-permute-start.2) | collective-permute-done | bytes 1048608 | tf_op jit(solution)/shard_map/ppermute | solution.py:12
  70.8 2.3 %exponential_reduce_fusion.6 = f32[2048]{0:T(1024)S(1)} fusion(f32[2,512]{1,0:T(2,128)S(1)} %get-tuple-element.33, bf16[512,2,128]{0,2,1:T(8,128)(2,1)S(1)} %bitcast.154, bf16[2048,256]{1,0:T(8,128)(2,1)S(1)} %copy-done), kind=kOutput, calls=%fused_computation.6 | convolution fusion | flops 543160320 | bytes 1323008 | tf_op jit(solution)/shard_map/qhd,khd->hqk/dot_general | solution.py:24
  73.1 7.7 %collective-permute-start.4 = (bf16[2048,256]{0,1:T(8,128)(2,1)S(1)}, bf16[2048,256]{0,1:T(8,128)(2,1)S(1)}, u32[]{:S(2)}, u32[]{:S(2)}) collective-permute-start(bf16[2048,256]{0,1:T(8,128)(2,1)S(1)} %collective-permute-done.2), channel_id=1, source_target_pairs={{16,0},{32,16},{48,32},{64,48},{80,64},{96,80},{112,96},{128,112},... | collective-permute-start | bytes 3145736 | tf_op jit(solution)/shard_map/ppermute | solution.py:12
  83.2 2.3 %exponential_reduce_fusion.5 = f32[2048]{0:T(1024)S(1)} fusion(f32[2,512]{1,0:T(2,128)S(1)} %get-tuple-element.35, bf16[512,2,128]{0,2,1:T(8,128)(2,1)S(1)} %bitcast.146, bf16[2048,256]{1,0:T(8,128)(2,1)S(1)} %copy-done), kind=kOutput, calls=%fused_computation.5 | convolution fusion | flops 543160320 | bytes 1323008 | tf_op jit(solution)/shard_map/qhd,khd->hqk/dot_general | solution.py:24
  85.5 2.3 %exponential_reduce_fusion.7 = f32[2048]{0:T(1024)S(1)} fusion(f32[2,512]{1,0:T(2,128)S(1)} %get-tuple-element.36, bf16[512,2,128]{0,2,1:T(8,128)(2,1)S(1)} %bitcast.144, bf16[2048,256]{1,0:T(8,128)(2,1)S(1)} %copy-done), kind=kOutput, calls=%fused_computation.7 | convolution fusion | flops 543160320 | bytes 1323008 | tf_op jit(solution)/shard_map/qhd,khd->hqk/dot_general | solution.py:24
  87.8 11.5 %collective-permute-done.4 = bf16[2048,256]{0,1:T(8,128)(2,1)S(1)} collective-permute-done((bf16[2048,256]{0,1:T(8,128)(2,1)S(1)}, bf16[2048,256]{0,1:T(8,128)(2,1)S(1)}, u32[]{:S(2)}, u32[]{:S(2)}) %collective-permute-start.4) | collective-permute-done | bytes 1048608 | tf_op jit(solution)/shard_map/ppermute | solution.py:12
  99.4 2.3 %exponential_reduce_fusion.2 = f32[2048]{0:T(1024)S(1)} fusion(f32[2,512]{1,0:T(2,128)S(1)} %get-tuple-element.37, bf16[512,2,128]{0,2,1:T(8,128)(2,1)S(1)} %bitcast.152, bf16[2048,256]{1,0:T(8,128)(2,1)S(1)} %copy-done), kind=kOutput, calls=%fused_computation.2 | convolution fusion | flops 543160320 | bytes 1323008 | tf_op jit(solution)/shard_map/qhd,khd->hqk/dot_general | solution.py:24
  104.1 2.3 %exponential_reduce_fusion.1 = f32[2048]{0:T(1024)S(1)} fusion(f32[2,512]{1,0:T(2,128)S(1)} %get-tuple-element.39, bf16[512,2,128]{0,2,1:T(8,128)(2,1)S(1)} %bitcast.150, bf16[2048,256]{1,0:T(8,128)(2,1)S(1)} %copy-done), kind=kOutput, calls=%fused_computation.1 | convolution fusion | flops 543160320 | bytes 1323008 | tf_op jit(solution)/shard_map/qhd,khd->hqk/dot_general | solution.py:24
  106.4 2.3 %exponential_reduce_fusion.3 = f32[2048]{0:T(1024)S(1)} fusion(f32[2,512]{1,0:T(2,128)S(1)} %get-tuple-element.40, bf16[512,2,128]{0,2,1:T(8,128)(2,1)S(1)} %bitcast.147, bf16[2048,256]{1,0:T(8,128)(2,1)S(1)} %copy-done), kind=kOutput, calls=%fused_computation.3 | convolution fusion | flops 543160320 | bytes 1323008 | tf_op jit(solution)/shard_map/qhd,khd->hqk/dot_general | solution.py:24
  108.7 32.5 %all-reduce = f32[2048]{0:T(1024)S(1)} all-reduce(f32[2048]{0:T(1024)S(1)} %multiply_add_fusion), channel_id=2, replica_groups=mesh['ctx'=16,'head'=16] {'head'}, use_global_device_ids=true, to_apply=%region_16.17.clone | all-reduce | flops 2048 | bytes 16384
  (28 shorter events, 12.1 us)
Async XLA Ops:
  0.0 15.4 %copy-start = (bf16[2048,256]{1,0:T(8,128)(2,1)S(1)}, bf16[2048,256]{1,0:T(8,128)(2,1)}, u32[]{:S(2)}) copy-start(bf16[2048,256]{1,0:T(8,128)(2,1)} %param.4) | copy-start | bytes 3145732
  0.0 11.5 %copy-start.1 = (bf16[2,2048]{1,0:T(2,128)(2,1)S(1)}, bf16[2,2048]{1,0:T(2,128)(2,1)}, u32[]{:S(2)}) copy-start(bf16[2,2048]{1,0:T(2,128)(2,1)} %param.6) | copy-start | bytes 24580
  0.0 29.6 %collective-permute-start.1 = (bf16[2,2048]{1,0:T(2,128)(2,1)}, bf16[2,2048]{1,0:T(2,128)(2,1)S(1)}, u32[]{:S(2)}, u32[]{:S(2)}) collective-permute-start(bf16[2,2048]{1,0:T(2,128)(2,1)} %param.6), channel_id=1, source_target_pairs={{16,0},{32,16},{48,32},{64,48},{80,64},{96,80},{112,96},{128,112},... | collective-permute-start | bytes 24584 | tf_op jit(solution)/shard_map/ppermute | solution.py:12
  8.9 32.8 %collective-permute-start = (bf16[2048,256]{0,1:T(8,128)(2,1)S(1)}, bf16[2048,256]{0,1:T(8,128)(2,1)S(1)}, u32[]{:S(2)}, u32[]{:S(2)}) collective-permute-start(bf16[2048,256]{0,1:T(8,128)(2,1)S(1)} %copy.58), channel_id=1, source_target_pairs={{16,0},{32,16},{48,32},{64,48},{80,64},{96,80},{112,96},{128,112},... | collective-permute-start | bytes 3145736 | tf_op jit(solution)/shard_map/ppermute | solution.py:12
  11.6 0.7 copy-start.2
  25.1 3.3 %copy-start.3 = (u32[256]{0:T(256)S(1)}, u32[256]{0:T(256)}, u32[]{:S(2)}) copy-start(u32[256]{0:T(256)} %constant.20) | copy-start | bytes 3076
  29.6 5.1 %collective-permute-start.3 = (bf16[2,2048]{1,0:T(2,128)(2,1)S(1)}, bf16[2,2048]{1,0:T(2,128)(2,1)S(1)}, u32[]{:S(2)}, u32[]{:S(2)}) collective-permute-start(bf16[2,2048]{1,0:T(2,128)(2,1)S(1)} %collective-permute-done.1), channel_id=1, source_target_pairs={{16,0},{32,16},{48,32},{64,48},{80,64},{96,80},{112,96},{128,112},... | collective-permute-start | bytes 24584 | tf_op jit(solution)/shard_map/ppermute | solution.py:12
  34.7 7.0 %collective-permute-start.5 = (bf16[2,2048]{1,0:T(2,128)(2,1)S(1)}, bf16[2,2048]{1,0:T(2,128)(2,1)S(1)}, u32[]{:S(2)}, u32[]{:S(2)}) collective-permute-start(bf16[2,2048]{1,0:T(2,128)(2,1)S(1)} %collective-permute-done.3), channel_id=1, source_target_pairs={{16,0},{32,16},{48,32},{64,48},{80,64},{96,80},{112,96},{128,112},... | collective-permute-start | bytes 24584 | tf_op jit(solution)/shard_map/ppermute | solution.py:12
  44.1 26.6 %collective-permute-start.2 = (bf16[2048,256]{0,1:T(8,128)(2,1)S(1)}, bf16[2048,256]{0,1:T(8,128)(2,1)S(1)}, u32[]{:S(2)}, u32[]{:S(2)}) collective-permute-start(bf16[2048,256]{0,1:T(8,128)(2,1)S(1)} %collective-permute-done), channel_id=1, source_target_pairs={{16,0},{32,16},{48,32},{64,48},{80,64},{96,80},{112,96},{128,112},... | collective-permute-start | bytes 3145736 | tf_op jit(solution)/shard_map/ppermute | solution.py:12
  73.1 26.2 %collective-permute-start.4 = (bf16[2048,256]{0,1:T(8,128)(2,1)S(1)}, bf16[2048,256]{0,1:T(8,128)(2,1)S(1)}, u32[]{:S(2)}, u32[]{:S(2)}) collective-permute-start(bf16[2048,256]{0,1:T(8,128)(2,1)S(1)} %collective-permute-done.2), channel_id=1, source_target_pairs={{16,0},{32,16},{48,32},{64,48},{80,64},{96,80},{112,96},{128,112},... | collective-permute-start | bytes 3145736 | tf_op jit(solution)/shard_map/ppermute | solution.py:12
where the time goes:
time: 142 us
  matrix products  40.6 us (29%)
  starting transfers between devices  34 us (24%)
  blocking collectives  32.5 us (23%)
  waiting for transfers between devices  27 us (19%)
  local copies, waits for them, and re-layouts  3.6 us (3%)
  other arithmetic  3.16 us (2%)
    dot_general x16, matrix products, block_mass(): jnp.einsum('qhd,khd->hqk', query_heads[first_row:first_row + block_size],...  40.6 us
    ppermute x6, starting transfers between devices, from_behind(): lax.ppermute(value, axis, [(source, source + steps) for source in range(l...  34 us
    unnamed x1, blocking collectives  32.5 us
    ppermute x6, waiting for transfers between devices, from_behind(): lax.ppermute(value, axis, [(source, source + steps) for source in range(l...  27 us
    unnamed x11, local copies, waits for them, and re-layouts  3.27 us
    le x2, other arithmetic, block_mass(): key_index[None, :] <= offsets[first_row:first_row + block_size, None]  3.1 us
  transfers between devices with their start and end apart: 6, of which 4 were waited for; matrix products, arithmetic and copies ran while one was open for 23% of the time, Pallas kernels for 0%

commit v1 on v0

v1 whole, which is shorter than its diff:
```python
import functools
import math

import jax
import jax.numpy as jnp
from jax import lax
from jax.experimental import pallas as pl
from jax.experimental.pallas import tpu as pltpu
from jax.sharding import PartitionSpec as P

HD = 128
LANES = 128
LOG2E = math.log2(math.e)
SCORE_SCALE = LOG2E / math.sqrt(HD)
DEAD = 1e30
Q_TILE = 256
CONTRACT_LAST = (((1,), (1,)), ((), ()))
VMEM_LIMIT = 40 * 2**20


def role_of_device():
    return lax.rem(lax.axis_index("head"), 2)


def prepare_kernel(q_ref, k_ref, lse_ref, x_ref, za_ref, zb_ref, lse_wide, lse_rows, sems):
    rows = q_ref.shape[0]
    lse_count = rows // LANES
    role = role_of_device()

    def arrange(moving, fixed):
        copies = [
            pltpu.make_async_copy(moving.at[:, :HD], x_ref.at[:rows], sems.at[0]),
            pltpu.make_async_copy(moving.at[:, HD:], x_ref.at[rows : 2 * rows], sems.at[1]),
            pltpu.make_async_copy(fixed.at[:, :HD], za_ref.at[:rows], sems.at[2]),
            pltpu.make_async_copy(fixed.at[:, HD:], zb_ref.at[:rows], sems.at[3]),
        ]
        for copy in copies:
            copy.start()
        lse_wide[...] = lse_ref[...].astype(jnp.float32)
        wide = []
        for head in range(2):
            for part in range(lse_count):
                wide.append(lse_wide[head : head + 1, part * LANES : (part + 1) * LANES])
        lse_rows[...] = jnp.concatenate(wide, axis=0).astype(jnp.bfloat16)
        small = [
            pltpu.make_async_copy(lse_rows, x_ref.at[2 * rows :], sems.at[4]),
            pltpu.make_async_copy(lse_rows.at[:lse_count], za_ref.at[rows:], sems.at[5]),
            pltpu.make_async_copy(lse_rows.at[lse_count:], zb_ref.at[rows:], sems.at[6]),
        ]
        for copy in small:
            copy.start()
        for copy in copies + small:
            copy.wait()

    pl.when(role == 0)(lambda: arrange(q_ref, k_ref))
    pl.when(role == 1)(lambda: arrange(k_ref, q_ref))


def prepare(key_rows, query_rows, row_lse):
    rows = query_rows.shape[0]
    lse_count = rows // LANES
    return pl.pallas_call(
        prepare_kernel,
        out_shape=(
            jax.ShapeDtypeStruct((2 * (rows + lse_count), HD), jnp.bfloat16),
            jax.ShapeDtypeStruct((rows + lse_count, HD), jnp.bfloat16),
            jax.ShapeDtypeStruct((rows + lse_count, HD), jnp.bfloat16),
        ),
        in_specs=[
            pl.BlockSpec(memory_space=pl.ANY),
            pl.BlockSpec(memory_space=pl.ANY),
            pl.BlockSpec(memory_space=pltpu.VMEM),
        ],
        out_specs=(pl.BlockSpec(memory_space=pl.ANY),) * 3,
        scratch_shapes=[
            pltpu.VMEM((2, rows), jnp.float32),
            pltpu.VMEM((2 * lse_count, LANES), jnp.bfloat16),
            pltpu.SemaphoreType.DMA((7,)),
        ],
        compiler_params=pltpu.CompilerParams(vmem_limit_bytes=VMEM_LIMIT),
        name="prepare",
    )(query_rows, key_rows, row_lse)


def add_pair(q_buf, k_buf, lse_buf, offsets, acc, is_first, is_live):
    rows = k_buf.shape[0]
    lse = lse_buf[...].astype(jnp.float32) * LOG2E
    lse = jnp.where(is_live, lse, DEAD)
    parts = Q_TILE // LANES
    for tile in range(q_buf.shape[0] // Q_TILE):
        scores = lax.dot_general(
            k_buf[...],
            q_buf[tile * Q_TILE : (tile + 1) * Q_TILE, :],
            CONTRACT_LAST,
            preferred_element_type=jnp.float32,
        )
        total = None
        for part in range(parts):
            row = tile * parts + part
            weights = jnp.exp2(
                scores[:, part * LANES : (part + 1) * LANES] * SCORE_SCALE - lse[row : row + 1, :]
            )
            if offsets is not None:
                key_index = lax.broadcasted_iota(jnp.int32, (rows, LANES), 0)
                weights = jnp.where(key_index <= offsets[row : row + 1, :], weights, 0.0)
            total = weights if total is None else total + weights
        if is_first and tile == 0:
            acc[...] = total
        else:
            acc[...] += total


def write_mass(acc, out_ref):
    for part in range(out_ref.shape[0]):
        turned = acc[part * LANES : (part + 1) * LANES, :].T
        out_ref[part : part + 1, :] = jnp.sum(turned, axis=0, keepdims=True)


def mass_kernel(jobs, n_arrays, n_small, finish, has_offsets, *refs):
    arrays = refs[:n_arrays]
    small = refs[n_arrays : n_arrays + n_small]
    n_out = 1 + max(job["out"] for job in jobs) if finish is None else 2
    outs = refs[n_arrays + n_small : n_arrays + n_small + n_out]
    q_buf, k_buf, lse_buf, acc, sems = refs[n_arrays + n_small + n_out :]
    rows = q_buf.shape[1]
    lse_count = lse_buf.shape[1]
    role = role_of_device()
    shard = lax.axis_index("ctx")
    shards = lax.axis_size("ctx")

    def copies_of(number, x_is_query):
        job = jobs[number]
        x, z = arrays[job["x"]], arrays[job["z"]]
        x_at, z_at = job["x_head"] * rows, job["z_head"] * rows
        x_lse = 2 * rows + job["x_head"] * lse_count if x.shape[0] > 2 * rows else rows
        z_lse = 2 * rows + job["z_head"] * lse_count if z.shape[0] > 2 * rows else rows
        query, q_at, lse_at, key, k_at = (
            (x, x_at, x_lse, z, z_at) if x_is_query else (z, z_at, z_lse, x, x_at)
        )
        return [
            pltpu.make_async_copy(key.at[pl.ds(k_at, rows)], k_buf.at[number], sems.at[number, 0]),
            pltpu.make_async_copy(
                query.at[pl.ds(q_at, rows)], q_buf.at[number], sems.at[number, 1]
            ),
            pltpu.make_async_copy(
                query.at[pl.ds(lse_at, lse_count)], lse_buf.at[number], sems.at[number, 2]
            ),
        ]

    def start_all(x_is_query):
        for number in range(len(jobs)):
            for copy in copies_of(number, x_is_query):
                copy.start()

    pl.when(role == 0)(lambda: start_all(True))
    pl.when(role == 1)(lambda: start_all(False))
    seen = set()
    for number, job in enumerate(jobs):
        for copy in copies_of(number, True):
            copy.wait()
        steps = jnp.where(role == 0, job["x_steps"], job["z_steps"])
        add_pair(
            q_buf.at[number],
            k_buf.at[number],
            lse_buf.at[number],
            small[0][...] if has_offsets else None,
            acc,
            job["out"] not in seen,
            shard + steps < shards,
        )
        seen.add(job["out"])
        if number + 1 == len(jobs) or jobs[number + 1]["out"] != job["out"]:
            write_mass(acc, outs[job["out"]])
    if finish is not None:
        finish(role, small, outs)


def mass_call(name, arrays, jobs, small=(), finish=None, has_offsets=False):
    rows = 2048 if not arrays else arrays[-1].shape[0] * LANES // (LANES + 1)
    lse_count = rows // LANES
    n_out = 1 + max(job["out"] for job in jobs) if finish is None else 2
    pairs = len(jobs) * rows * rows
    return pl.pallas_call(
        functools.partial(mass_kernel, jobs, len(arrays), len(small), finish, has_offsets),
        out_shape=tuple(
            jax.ShapeDtypeStruct((lse_count, LANES), jnp.float32) for _ in range(n_out)
        ),
        in_specs=[pl.BlockSpec(memory_space=pl.ANY)] * len(arrays)
        + [pl.BlockSpec(memory_space=pltpu.VMEM)] * len(small),
        out_specs=tuple(pl.BlockSpec(memory_space=pltpu.VMEM) for _ in range(n_out)),
        scratch_shapes=[
            pltpu.VMEM((len(jobs), rows, HD), jnp.bfloat16),
            pltpu.VMEM((len(jobs), rows, HD), jnp.bfloat16),
            pltpu.VMEM((len(jobs), lse_count, LANES), jnp.bfloat16),
            pltpu.VMEM((rows, LANES), jnp.float32),
            pltpu.SemaphoreType.DMA((len(jobs), 3)),
        ],
        compiler_params=pltpu.CompilerParams(vmem_limit_bytes=VMEM_LIMIT),
        cost_estimate=pl.CostEstimate(
            flops=2 * pairs * HD, transcendentals=pairs, bytes_accessed=len(jobs) * 2**20
        ),
        name=name,
    )(*arrays, *small)


def job(x, x_head, x_steps, z, z_head, z_steps, out=0):
    return dict(x=x, x_head=x_head, x_steps=x_steps, z=z, z_head=z_head, z_steps=z_steps, out=out)


def combine(role, small, outs):
    own, first, first_back, second, third = [ref[...] for ref in small]
    last = outs[0][...] + third
    is_query_mover = role == 0
    outs[0][...] = jnp.where(is_query_mover, last, last + second)
    outs[1][...] = own + first_back + jnp.where(is_query_mover, first + second, 0.0)


def move(value, mesh_shape, steps_of_role):
    shards, heads = mesh_shape
    pairs = []
    for shard in range(shards):
        for head in range(heads):
            steps = steps_of_role[head % 2]
            if steps != 0 and 0 <= shard + steps < shards:
                pairs.append((shard * heads + head, (shard + steps) * heads + head))
    return lax.ppermute(value, ("ctx", "head"), pairs)


def on_device(mesh_shape, key_rows, query_rows, row_lse, query_offsets):
    rows = query_rows.shape[0]
    x0, za0, zb0 = prepare(key_rows, query_rows, row_lse)
    x1 = move(x0, mesh_shape, (-1, 1))
    za1 = move(za0, mesh_shape, (1, -1))
    offsets = query_offsets.reshape(rows // LANES, LANES)
    (own,) = mass_call(
        "own",
        [x0, za0, zb0],
        [job(0, 0, 0, 1, 0, 0), job(0, 1, 0, 2, 0, 0)],
        small=(offsets,),
        has_offsets=True,
    )
    x1, own = lax.optimization_barrier((x1, own))
    x2 = move(x1, mesh_shape, (-1, 1))
    za1, x1 = lax.optimization_barrier((za1, x1))
    (first,) = mass_call(
        "first", [x1, za0, zb0], [job(0, 0, 1, 1, 0, 0), job(0, 1, 1, 2, 0, 0)]
    )
    first_back = move(first, mesh_shape, (0, -1))
    zb0, first = lax.optimization_barrier((zb0, first))
    zb1 = move(zb0, mesh_shape, (1, -1))
    second, third = mass_call(
        "second",
        [x2, za0, zb0, za1],
        [job(0, 0, 2, 1, 0, 0), job(0, 1, 2, 2, 0, 0), job(0, 0, 2, 3, 0, 1, out=1)],
    )
    back, local = mass_call(
        "third",
        [x2, zb1],
        [job(0, 1, 2, 1, 0, 1)],
        small=(own, first, first_back, second, third),
        finish=combine,
    )
    local = local + move(back, mesh_shape, (-1, -2))
    spread = lax.all_to_all(local, "head", 0, 0, tiled=True)
    return jnp.sum(spread, axis=0)


def solution(mesh):
    mesh_shape = (mesh.shape["ctx"], mesh.shape["head"])
    in_specs = (P("ctx", "head"), P("ctx", "head"), P("head", "ctx"), P("ctx"))
    out_specs = P(("ctx", "head"))
    return jax.shard_map(
        functools.partial(on_device, mesh_shape),
        mesh=mesh,
        in_specs=in_specs,
        out_specs=out_specs,
        check_vma=False,
    )
```

time: 142 us -> 89.2 us (0.63)
  matrix products: 40.6 us -> 0 us
  Pallas kernels: 0 us -> 25.1 us
  blocking collectives: 32.5 us -> 13.8 us
  starting transfers between devices: 34 us -> 24 us
  waiting for transfers between devices: 27 us -> 22.1 us
  other arithmetic: 3.16 us -> 0.55 us
    dot_general x16 -> x0, matrix products: 40.6 us -> none  [block_mass(): jnp.einsum('qhd,khd->hqk', query_heads[first_row:first_row + block_size],...]
    unnamed x1 -> x0, blocking collectives: 32.5 us -> none
    pallas_call x0 -> x5, Pallas kernels: none -> 25.1 us  [the longest x4 24.6 us: mass_call(): pl.pallas_call(functools.partial(mass_kernel, jobs, len(arrays), len(smal...]
    all_to_all x0 -> x1, blocking collectives: none -> 13.8 us  [on_device(): spread = lax.all_to_all(local, 'head', 0, 0, tiled=True)]
    ppermute x6, starting transfers between devices: 34 us -> 24 us  [move(): return lax.ppermute(value, ('ctx', 'head'), pairs)]
    ppermute x6, waiting for transfers between devices: 27 us -> 22.1 us  [move(): return lax.ppermute(value, ('ctx', 'head'), pairs)]
    le x2 -> x0, other arithmetic: 3.1 us -> none  [block_mass(): key_index[None, :] <= offsets[first_row:first_row + block_size, None]]
    unnamed x11 -> x8, local copies, waits for them, and re-layouts: 3.27 us -> 3.15 us
  transfers between devices with their start and end apart: 6 -> 6, of which waited for: 4 -> 3; matrix products, arithmetic and copies ran while one was open for 23% -> 0% of each run, Pallas kernels for 0% -> 25%
where the time goes in v1:
time: 89.2 us; the launch traced here: 88.8 us
  Pallas kernels  25.1 us (28%)
  starting transfers between devices  24 us (27%)
  waiting for transfers between devices  22.1 us (25%)
  blocking collectives  13.8 us (15%)
  local copies, waits for them, and re-layouts  3.15 us (4%)
    pallas_call x4, Pallas kernels, mass_call(): pl.pallas_call(functools.partial(mass_kernel, jobs, len(arrays), len(smal...  24.6 us
    ppermute x6, starting transfers between devices, move(): return lax.ppermute(value, ('ctx', 'head'), pairs)  24 us
    ppermute x6, waiting for transfers between devices, move(): return lax.ppermute(value, ('ctx', 'head'), pairs)  22.1 us
    all_to_all x1, blocking collectives, on_device(): spread = lax.all_to_all(local, 'head', 0, 0, tiled=True)  13.8 us
    unnamed x8, local copies, waits for them, and re-layouts  3.15 us
  transfers between devices with their start and end apart: 6, of which 3 were waited for; matrix products, arithmetic and copies ran while one was open for 0% of the time, Pallas kernels for 25%

profile of v1, /device:TPU:17, one launch (start us, length us, event | category | flops | bytes accessed | tf_op | source)
XLA Modules:
  0.0 88.8 jit_solution(7227883589750548682)
XLA Ops:
  0.0 0.0 copy-start
  0.0 1.2 %copy-done = bf16[2048,256]{1,0:T(8,128)(2,1)S(1)} copy-done((bf16[2048,256]{1,0:T(8,128)(2,1)S(1)}, bf16[2048,256]{1,0:T(8,128)(2,1)}, u32[]{:S(2)}) %copy-start) | copy-done | bytes 1048600
  1.2 1.2 %copy-done.1 = bf16[2048,256]{1,0:T(8,128)(2,1)S(1)} copy-done((bf16[2048,256]{1,0:T(8,128)(2,1)S(1)}, bf16[2048,256]{1,0:T(8,128)(2,1)}, u32[]{:S(2)}) %copy-start.1) | copy-done | bytes 1048600
  2.5 0.7 copy-done.2
  3.2 0.5 prepare.1
  3.6 3.5 %collective-permute-start = (bf16[4128,128]{1,0:T(8,128)(2,1)S(1)}, bf16[4128,128]{1,0:T(8,128)(2,1)S(1)}, u32[]{:S(2)}, u32[]{:S(2)}) collective-permute-start(bf16[4128,128]{1,0:T(8,128)(2,1)S(1)} %get-tuple-element.18.refs_0_), channel_id=1, source_target_pairs={{1,17},{3,19},{5,21},{7,23},{9,25},{11,27},{13,29},{15,31},{16,0},... | collective-permute-start | bytes 3170312 | tf_op jit(solution)/shard_map/ppermute | solution.py:226
  7.2 0.0 copy-done.3
  7.2 8.7 %own.1.refs_2_ = f32[16,128]{1,0:T(8,128)S(1)} custom-call(bf16[4128,128]{1,0:T(8,128)(2,1)S(1)} %get-tuple-element.18.refs_0_, bf16[2064,128]{1,0:T(8,128)(2,1)S(1)} %get-tuple-element.19.refs_1_, bf16[2064,128]{1,0:T(8,128)(2,1)S(1)} %get-tuple-element.23.refs_2_, s32[16,128]{1,0:T(8,128)S(1)} %bitcast.4), custom_call_target="tpu_custom_call" | custom-call | flops 2147483648 | bytes 2097152 | tf_op jit(solution)/shard_map/own/pallas_call | solution.py:183
  15.9 7.2 %collective-permute-done.refs_0_ = bf16[4128,128]{1,0:T(8,128)(2,1)S(1)} collective-permute-done((bf16[4128,128]{1,0:T(8,128)(2,1)S(1)}, bf16[4128,128]{1,0:T(8,128)(2,1)S(1)}, u32[]{:S(2)}, u32[]{:S(2)}) %collective-permute-start) | collective-permute-done | bytes 1056800 | tf_op jit(solution)/shard_map/ppermute | solution.py:226
  23.2 1.9 %collective-permute-start.1 = (bf16[4128,128]{1,0:T(8,128)(2,1)S(1)}, bf16[4128,128]{1,0:T(8,128)(2,1)S(1)}, u32[]{:S(2)}, u32[]{:S(2)}) collective-permute-start(bf16[4128,128]{1,0:T(8,128)(2,1)S(1)} %collective-permute-done.refs_0_), channel_id=1, source_target_pairs={{1,17},{3,19},{5,21},{7,23},{9,25},{11,27},{13,29},{15,31},{16,0},... | collective-permute-start | bytes 3170312 | tf_op jit(solution)/shard_map/ppermute | solution.py:226
  25.1 7.0 %collective-permute-start.2 = (bf16[2064,128]{1,0:T(8,128)(2,1)S(1)}, bf16[2064,128]{1,0:T(8,128)(2,1)S(1)}, u32[]{:S(2)}, u32[]{:S(2)}) collective-permute-start(bf16[2064,128]{1,0:T(8,128)(2,1)S(1)} %get-tuple-element.19.refs_1_), channel_id=1, source_target_pairs={{0,16},{2,18},{4,20},{6,22},{8,24},{10,26},{12,28},{14,30},{16,32}... | collective-permute-start | bytes 1585160 | tf_op jit(solution)/shard_map/ppermute | solution.py:226
  32.1 11.5 %collective-permute-done.2.refs_3_ = bf16[2064,128]{1,0:T(8,128)(2,1)S(1)} collective-permute-done((bf16[2064,128]{1,0:T(8,128)(2,1)S(1)}, bf16[2064,128]{1,0:T(8,128)(2,1)S(1)}, u32[]{:S(2)}, u32[]{:S(2)}) %collective-permute-start.2) | collective-permute-done | bytes 528416 | tf_op jit(solution)/shard_map/ppermute | solution.py:226
  43.6 5.4 %first.1.refs_3_ = f32[16,128]{1,0:T(8,128)S(1)} custom-call(bf16[4128,128]{1,0:T(8,128)(2,1)S(1)} %collective-permute-done.refs_0_, bf16[2064,128]{1,0:T(8,128)(2,1)S(1)} %get-tuple-element.19.refs_1_, bf16[2064,128]{1,0:T(8,128)(2,1)S(1)} %get-tuple-element.23.refs_2_), custom_call_target="tpu_custom_call" | custom-call | flops 2147483648 | bytes 2097152 | tf_op jit(solution)/shard_map/first/pallas_call | solution.py:183
  49.0 7.7 %collective-permute-start.3 = (bf16[2064,128]{1,0:T(8,128)(2,1)S(1)}, bf16[2064,128]{1,0:T(8,128)(2,1)S(1)}, u32[]{:S(2)}, u32[]{:S(2)}) collective-permute-start(bf16[2064,128]{1,0:T(8,128)(2,1)S(1)} %get-tuple-element.23.refs_2_), channel_id=1, source_target_pairs={{0,16},{2,18},{4,20},{6,22},{8,24},{10,26},{12,28},{14,30},{16,32}... | collective-permute-start | bytes 1585160 | tf_op jit(solution)/shard_map/ppermute | solution.py:226
  56.7 1.9 %collective-permute-start.4 = (f32[16,128]{1,0:T(8,128)S(1)}, f32[16,128]{1,0:T(8,128)S(1)}, u32[]{:S(2)}, u32[]{:S(2)}) collective-permute-start(f32[16,128]{1,0:T(8,128)S(1)} %first.1.refs_3_), channel_id=1, source_target_pairs={{17,1},{19,3},{21,5},{23,7},{25,9},{27,11},{29,13},{31,15},{33,17}... | collective-permute-start | bytes 24584 | tf_op jit(solution)/shard_map/ppermute | solution.py:226
  58.6 0.0 collective-permute-done.1.refs_0_
  58.6 7.8 %second.1 = (f32[16,128]{1,0:T(8,128)S(1)}, f32[16,128]{1,0:T(8,128)S(1)}) custom-call(bf16[4128,128]{1,0:T(8,128)(2,1)S(1)} %collective-permute-done.1.refs_0_, bf16[2064,128]{1,0:T(8,128)(2,1)S(1)} %get-tuple-element.19.refs_1_, bf16[2064,128]{1,0:T(8,128)(2,1)S(1)} %get-tuple-element.23.refs_2_, bf16[2064,128]{1,0:T(8,128)(2,1)S(1)} %collective-permute-done.2.refs_3_), custom_call_target="tpu_custom_call" | custom-call | flops 3221225472 | bytes 3145728 | tf_op jit(solution)/shard_map/second/pallas_call | solution.py:183
  66.5 0.0 collective-permute-done.4.refs_4_
  66.5 0.0 collective-permute-done.3.refs_1_
  66.5 2.7 %third.1 = (f32[16,128]{1,0:T(8,128)S(1)}, f32[16,128]{1,0:T(8,128)S(1)}) custom-call(bf16[4128,128]{1,0:T(8,128)(2,1)S(1)} %collective-permute-done.1.refs_0_, bf16[2064,128]{1,0:T(8,128)(2,1)S(1)} %collective-permute-done.3.refs_1_, f32[16,128]{1,0:T(8,128)S(1)} %own.1.refs_2_, f32[16,128]{1,0:T(8,128)S(1)} %first.1.refs_3_, ...), custom_call_target="tpu_custom_call" | custom-call | flops 1073741824 | bytes 1048576 | tf_op jit(solution)/shard_map/third/pallas_call | solution.py:183
  69.2 1.9 %collective-permute-start.5 = (f32[16,128]{1,0:T(8,128)S(1)}, f32[16,128]{1,0:T(8,128)S(1)}, u32[]{:S(2)}, u32[]{:S(2)}) collective-permute-start(f32[16,128]{1,0:T(8,128)S(1)} %get-tuple-element.30), channel_id=1, source_target_pairs={{16,0},{18,2},{20,4},{22,6},{24,8},{26,10},{28,12},{30,14},{32,16}... | collective-permute-start | bytes 24584 | tf_op jit(solution)/shard_map/ppermute | solution.py:226
  71.1 3.4 %collective-permute-done.5 = f32[16,128]{1,0:T(8,128)S(1)} collective-permute-done((f32[16,128]{1,0:T(8,128)S(1)}, f32[16,128]{1,0:T(8,128)S(1)}, u32[]{:S(2)}, u32[]{:S(2)}) %collective-permute-start.5) | collective-permute-done | bytes 8224 | tf_op jit(solution)/shard_map/ppermute | solution.py:226
  74.5 13.8 %all_to_all.9 = f32[16,1,128]{2,1,0:T(1,128)S(1)} all-to-all(f32[16,1,128]{2,1,0:T(1,128)S(1)} %bitcast.5), channel_id=1, replica_groups=mesh['ctx'=16,'head'=16] {'head'}, dimensions={0} | all-to-all | bytes 16384 | tf_op jit(solution)/shard_map/all_to_all | solution.py:264
  88.2 0.5 reduce_sum.9
  (4 shorter events, 0.0 us)
Async XLA Ops:
  0.0 1.2 %copy-start = (bf16[2048,256]{1,0:T(8,128)(2,1)S(1)}, bf16[2048,256]{1,0:T(8,128)(2,1)}, u32[]{:S(2)}) copy-start(bf16[2048,256]{1,0:T(8,128)(2,1)} %q_ref.1) | copy-start | bytes 3145732
  1.2 1.2 %copy-start.1 = (bf16[2048,256]{1,0:T(8,128)(2,1)S(1)}, bf16[2048,256]{1,0:T(8,128)(2,1)}, u32[]{:S(2)}) copy-start(bf16[2048,256]{1,0:T(8,128)(2,1)} %k_ref.1) | copy-start | bytes 3145732
  2.5 0.7 copy-start.2
  3.1 4.0 %copy-start.3 = (s32[2048]{0:T(1024)S(1)}, s32[2048]{0:T(1024)}, u32[]{:S(2)}) copy-start(s32[2048]{0:T(1024)} %param.7) | copy-start | bytes 24580
  3.6 19.5 %collective-permute-start = (bf16[4128,128]{1,0:T(8,128)(2,1)S(1)}, bf16[4128,128]{1,0:T(8,128)(2,1)S(1)}, u32[]{:S(2)}, u32[]{:S(2)}) collective-permute-start(bf16[4128,128]{1,0:T(8,128)(2,1)S(1)} %get-tuple-element.18.refs_0_), channel_id=1, source_target_pairs={{1,17},{3,19},{5,21},{7,23},{9,25},{11,27},{13,29},{15,31},{16,0},... | collective-permute-start | bytes 3170312 | tf_op jit(solution)/shard_map/ppermute | solution.py:226
  23.2 35.5 %collective-permute-start.1 = (bf16[4128,128]{1,0:T(8,128)(2,1)S(1)}, bf16[4128,128]{1,0:T(8,128)(2,1)S(1)}, u32[]{:S(2)}, u32[]{:S(2)}) collective-permute-start(bf16[4128,128]{1,0:T(8,128)(2,1)S(1)} %collective-permute-done.refs_0_), channel_id=1, source_target_pairs={{1,17},{3,19},{5,21},{7,23},{9,25},{11,27},{13,29},{15,31},{16,0},... | collective-permute-start | bytes 3170312 | tf_op jit(solution)/shard_map/ppermute | solution.py:226
  25.1 18.5 %collective-permute-start.2 = (bf16[2064,128]{1,0:T(8,128)(2,1)S(1)}, bf16[2064,128]{1,0:T(8,128)(2,1)S(1)}, u32[]{:S(2)}, u32[]{:S(2)}) collective-permute-start(bf16[2064,128]{1,0:T(8,128)(2,1)S(1)} %get-tuple-element.19.refs_1_), channel_id=1, source_target_pairs={{0,16},{2,18},{4,20},{6,22},{8,24},{10,26},{12,28},{14,30},{16,32}... | collective-permute-start | bytes 1585160 | tf_op jit(solution)/shard_map/ppermute | solution.py:226
  49.0 17.5 %collective-permute-start.3 = (bf16[2064,128]{1,0:T(8,128)(2,1)S(1)}, bf16[2064,128]{1,0:T(8,128)(2,1)S(1)}, u32[]{:S(2)}, u32[]{:S(2)}) collective-permute-start(bf16[2064,128]{1,0:T(8,128)(2,1)S(1)} %get-tuple-element.23.refs_2_), channel_id=1, source_target_pairs={{0,16},{2,18},{4,20},{6,22},{8,24},{10,26},{12,28},{14,30},{16,32}... | collective-permute-start | bytes 1585160 | tf_op jit(solution)/shard_map/ppermute | solution.py:226
  56.7 9.8 %collective-permute-start.4 = (f32[16,128]{1,0:T(8,128)S(1)}, f32[16,128]{1,0:T(8,128)S(1)}, u32[]{:S(2)}, u32[]{:S(2)}) collective-permute-start(f32[16,128]{1,0:T(8,128)S(1)} %first.1.refs_3_), channel_id=1, source_target_pairs={{17,1},{19,3},{21,5},{23,7},{25,9},{27,11},{29,13},{31,15},{33,17}... | collective-permute-start | bytes 24584 | tf_op jit(solution)/shard_map/ppermute | solution.py:226
  69.2 5.3 %collective-permute-start.5 = (f32[16,128]{1,0:T(8,128)S(1)}, f32[16,128]{1,0:T(8,128)S(1)}, u32[]{:S(2)}, u32[]{:S(2)}) collective-permute-start(f32[16,128]{1,0:T(8,128)S(1)} %get-tuple-element.30), channel_id=1, source_target_pairs={{16,0},{18,2},{20,4},{22,6},{24,8},{26,10},{28,12},{30,14},{32,16}... | collective-permute-start | bytes 24584 | tf_op jit(solution)/shard_map/ppermute | solution.py:226

commit v2 on v1

v2 whole, which is shorter than its diff:
```python
import functools
import math

import jax
import jax.numpy as jnp
from jax import lax
from jax.experimental import pallas as pl
from jax.experimental.pallas import tpu as pltpu
from jax.sharding import PartitionSpec as P

HD = 128
LANES = 128
LOG2E = math.log2(math.e)
SCORE_SCALE = LOG2E / math.sqrt(HD)
DEAD = 1e30
Q_TILE = 256
CONTRACT_LAST = (((1,), (1,)), ((), ()))
VMEM_LIMIT = 40 * 2**20


def role_of_device():
    return lax.rem(lax.axis_index("head"), 2)


def prepare_kernel(q_ref, k_ref, lse_ref, xa_ref, xb_ref, za_ref, zb_ref, lse_rows, sems):
    rows = q_ref.shape[0]
    lse_count = rows // LANES
    role = role_of_device()

    def arrange(moving, fixed):
        copies = [
            pltpu.make_async_copy(moving.at[:, :HD], xa_ref.at[:rows], sems.at[0]),
            pltpu.make_async_copy(moving.at[:, HD:], xb_ref.at[:rows], sems.at[1]),
            pltpu.make_async_copy(fixed.at[:, :HD], za_ref.at[:rows], sems.at[2]),
            pltpu.make_async_copy(fixed.at[:, HD:], zb_ref.at[:rows], sems.at[3]),
        ]
        for copy in copies:
            copy.start()
        lse = lse_ref[...].astype(jnp.float32)
        for head in range(2):
            pieces = [
                lse[head : head + 1, part * LANES : (part + 1) * LANES]
                for part in range(lse_count)
            ]
            lse_rows[head] = jnp.concatenate(pieces, axis=0).astype(jnp.bfloat16)
        for number, (ref, head) in enumerate(
            [(xa_ref, 0), (xb_ref, 1), (za_ref, 0), (zb_ref, 1)]
        ):
            copies.append(
                pltpu.make_async_copy(lse_rows.at[head], ref.at[rows:], sems.at[4 + number])
            )
            copies[-1].start()
        for copy in copies:
            copy.wait()

    pl.when(role == 0)(lambda: arrange(q_ref, k_ref))
    pl.when(role == 1)(lambda: arrange(k_ref, q_ref))


def prepare(key_rows, query_rows, row_lse):
    rows = query_rows.shape[0]
    lse_count = rows // LANES
    half = jax.ShapeDtypeStruct((rows + lse_count, HD), jnp.bfloat16)
    return pl.pallas_call(
        prepare_kernel,
        out_shape=(half,) * 4,
        in_specs=[
            pl.BlockSpec(memory_space=pltpu.HBM),
            pl.BlockSpec(memory_space=pltpu.HBM),
            pl.BlockSpec(memory_space=pltpu.VMEM),
        ],
        out_specs=(pl.BlockSpec(memory_space=pl.ANY),) * 4,
        scratch_shapes=[
            pltpu.VMEM((2, lse_count, LANES), jnp.bfloat16),
            pltpu.SemaphoreType.DMA((8,)),
        ],
        compiler_params=pltpu.CompilerParams(vmem_limit_bytes=VMEM_LIMIT),
        name="prepare",
    )(
        pltpu.with_memory_space_constraint(query_rows, pltpu.HBM),
        pltpu.with_memory_space_constraint(key_rows, pltpu.HBM),
        row_lse,
    )


def add_pair(q_buf, k_buf, lse_buf, offsets, key_index, acc, is_first, is_live):
    lse = lse_buf[...].astype(jnp.float32) * LOG2E
    lse = jnp.where(is_live, lse, DEAD)
    parts = Q_TILE // LANES
    for tile in range(q_buf.shape[0] // Q_TILE):
        scores = lax.dot_general(
            k_buf[...],
            q_buf[tile * Q_TILE : (tile + 1) * Q_TILE, :],
            CONTRACT_LAST,
            preferred_element_type=jnp.float32,
        )
        total = None
        for part in range(parts):
            row = tile * parts + part
            weights = jnp.exp2(
                scores[:, part * LANES : (part + 1) * LANES] * SCORE_SCALE - lse[row : row + 1, :]
            )
            if offsets is not None:
                weights = jnp.where(key_index[...] <= offsets[row : row + 1, :], weights, 0.0)
            total = weights if total is None else total + weights
        if is_first and tile == 0:
            acc[...] = total
        else:
            acc[...] += total


def turned_mass(acc, count):
    parts = []
    for part in range(count):
        turned = acc[part * LANES : (part + 1) * LANES, :].T
        parts.append(jnp.sum(turned, axis=0, keepdims=True))
    return jnp.concatenate(parts, axis=0)


def mass_kernel(jobs, n_arrays, n_small, n_out, finish, is_own, *refs):
    arrays = refs[:n_arrays]
    small = refs[n_arrays : n_arrays + n_small]
    outs = refs[n_arrays + n_small : n_arrays + n_small + n_out]
    q_buf, k_buf, lse_buf, acc, key_index, sems = refs[n_arrays + n_small + n_out :]
    rows = q_buf.shape[1]
    lse_count = lse_buf.shape[1]
    role = role_of_device()
    shard = lax.axis_index("ctx")
    shards = lax.axis_size("ctx")

    def copies_of(number, x_is_query):
        x, z = arrays[jobs[number]["x"]], arrays[jobs[number]["z"]]
        query, key = (x, z) if x_is_query else (z, x)
        return [
            pltpu.make_async_copy(key.at[:rows], k_buf.at[number], sems.at[number, 0]),
            pltpu.make_async_copy(query.at[:rows], q_buf.at[number], sems.at[number, 1]),
            pltpu.make_async_copy(query.at[rows:], lse_buf.at[number], sems.at[number, 2]),
        ]

    def start_all(x_is_query):
        for number in range(len(jobs)):
            for copy in copies_of(number, x_is_query):
                copy.start()

    pl.when(role == 0)(lambda: start_all(True))
    pl.when(role == 1)(lambda: start_all(False))
    if is_own:
        key_index[...] = lax.broadcasted_iota(jnp.int32, key_index.shape, 0)
    masses = {}
    for number, job in enumerate(jobs):
        for copy in copies_of(number, True):
            copy.wait()
        steps = jnp.where(role == 0, job["x_steps"], job["z_steps"])
        add_pair(
            q_buf.at[number],
            k_buf.at[number],
            lse_buf.at[number],
            small[0][...] if is_own else None,
            key_index,
            acc,
            job["out"] not in masses,
            shard + steps < shards,
        )
        masses[job["out"]] = None
        if number + 1 == len(jobs) or jobs[number + 1]["out"] != job["out"]:
            masses[job["out"]] = turned_mass(acc, lse_count)
    results = [masses[number] for number in sorted(masses)]
    if finish is not None:
        results = finish(role, results, [ref[...] for ref in small])
    for out, result in zip(outs, results):
        out[...] = result


def mass_call(name, arrays, jobs, small=(), n_out=1, finish=None, is_own=False):
    padded = arrays[0].shape[0]
    rows = padded * LANES // (LANES + 1)
    lse_count = padded - rows
    pairs = len(jobs) * rows * rows
    return pl.pallas_call(
        functools.partial(mass_kernel, jobs, len(arrays), len(small), n_out, finish, is_own),
        out_shape=tuple(
            jax.ShapeDtypeStruct((lse_count, LANES), jnp.float32) for _ in range(n_out)
        ),
        in_specs=[pl.BlockSpec(memory_space=pl.ANY)] * len(arrays)
        + [pl.BlockSpec(memory_space=pltpu.VMEM)] * len(small),
        out_specs=tuple(pl.BlockSpec(memory_space=pltpu.VMEM) for _ in range(n_out)),
        scratch_shapes=[
            pltpu.VMEM((len(jobs), rows, HD), jnp.bfloat16),
            pltpu.VMEM((len(jobs), rows, HD), jnp.bfloat16),
            pltpu.VMEM((len(jobs), lse_count, LANES), jnp.bfloat16),
            pltpu.VMEM((rows, LANES), jnp.float32),
            pltpu.VMEM((rows if is_own else 8, LANES), jnp.int32),
            pltpu.SemaphoreType.DMA((len(jobs), 3)),
        ],
        compiler_params=pltpu.CompilerParams(vmem_limit_bytes=VMEM_LIMIT),
        cost_estimate=pl.CostEstimate(
            flops=2 * pairs * HD, transcendentals=pairs, bytes_accessed=len(jobs) * 2**20
        ),
        name=name,
    )(*arrays, *small)


def job(x, x_steps, z, z_steps, out=0):
    return dict(x=x, x_steps=x_steps, z=z, z_steps=z_steps, out=out)


def finish_middle(role, results, small):
    middle, last = results
    return [middle, last, middle + small[0]]


def finish_last(role, results, small):
    own_a, own_b, first, middle, last_a = small
    zero = jnp.zeros_like(first)
    back = results[0] + last_a + jnp.where(role == 0, middle, zero)
    local = own_a + own_b + jnp.where(role == 0, first, zero)
    return [back, local]


def move(value, mesh_shape, steps_of_role):
    shards, heads = mesh_shape
    pairs = []
    for shard in range(shards):
        for head in range(heads):
            steps = steps_of_role[head % 2]
            if steps != 0 and 0 <= shard + steps < shards:
                pairs.append((shard * heads + head, (shard + steps) * heads + head))
    return lax.ppermute(value, ("ctx", "head"), pairs)


def after(value, *done):
    return lax.optimization_barrier((value, *done))[0]


def on_device(mesh_shape, key_rows, query_rows, row_lse, query_offsets):
    rows = query_rows.shape[0]
    out, back = (-1, 1), (1, -1)
    xa0, xb0, za0, zb0 = prepare(key_rows, query_rows, row_lse)
    offsets = query_offsets.reshape(rows // LANES, LANES)
    xa1 = move(xa0, mesh_shape, out)
    xb1 = move(after(xb0, xa0), mesh_shape, out)
    za1 = move(za0, mesh_shape, back)
    (own_a,) = mass_call("own_a", [xa0, za0], [job(0, 0, 1, 0)], (offsets,), is_own=True)
    xa1 = after(xa1, own_a)
    xa2 = move(xa1, mesh_shape, out)
    (own_b,) = mass_call(
        "own_b", [after(xb0, xa1), zb0], [job(0, 0, 1, 0)], (offsets,), is_own=True
    )
    xb1 = after(xb1, own_b)
    xb2 = move(xb1, mesh_shape, out)
    zb1 = move(after(zb0, own_b), mesh_shape, back)
    (first,) = mass_call(
        "first", [after(xa1, za1), za0, xb1, zb0], [job(0, 1, 1, 0), job(2, 1, 3, 0)]
    )
    middle, last_a, send = mass_call(
        "middle",
        [xa2, xa1, za1, xb1, zb1],
        [job(0, 2, 2, 1, out=1), job(1, 1, 2, 1), job(3, 1, 4, 1)],
        (first,),
        n_out=3,
        finish=finish_middle,
    )
    near = move(send, mesh_shape, (0, -1))
    far, local = mass_call(
        "last",
        [xb2, zb1],
        [job(0, 2, 1, 1)],
        (own_a, own_b, first, middle, last_a),
        n_out=2,
        finish=finish_last,
    )
    local = local + near + move(far, mesh_shape, (-1, -2))
    spread = lax.all_to_all(local, "head", 0, 0, tiled=True)
    return jnp.sum(spread, axis=0)


def solution(mesh):
    mesh_shape = (mesh.shape["ctx"], mesh.shape["head"])
    in_specs = (P("ctx", "head"), P("ctx", "head"), P("head", "ctx"), P("ctx"))
    out_specs = P(("ctx", "head"))
    return jax.shard_map(
        functools.partial(on_device, mesh_shape),
        mesh=mesh,
        in_specs=in_specs,
        out_specs=out_specs,
        check_vma=False,
    )
```

time: 89.2 us -> 75.2 us (0.84)
  waiting for transfers between devices: 22.1 us -> 11.3 us
  blocking collectives: 13.8 us -> 11.3 us
  local copies, waits for them, and re-layouts: 3.15 us -> 0.7 us
  Pallas kernels: 25.1 us -> 27.3 us
    ppermute x6 -> x8, waiting for transfers between devices: 22.1 us -> 11.3 us  [move(): return lax.ppermute(value, ('ctx', 'head'), pairs)]
    unnamed x8 -> x4, local copies, waits for them, and re-layouts: 3.15 us -> 0.7 us
    all_to_all x1, blocking collectives: 13.8 us -> 11.3 us  [on_device(): spread = lax.all_to_all(local, 'head', 0, 0, tiled=True)]
    pallas_call x1, Pallas kernels: 0.47 us -> 1.6 us  [prepare(): pl.pallas_call(prepare_kernel, out_shape=(half,) * 4, in_specs=[pl.BlockS...]
    pallas_call x4 -> x5, Pallas kernels: 24.6 us -> 25.7 us  [mass_call(): pl.pallas_call(functools.partial(mass_kernel, jobs, len(arrays), len(smal...]
    ppermute x6 -> x8, starting transfers between devices: 24 us -> 23.5 us  [move(): return lax.ppermute(value, ('ctx', 'head'), pairs)]
  transfers between devices with their start and end apart: 6 -> 8, of which waited for: 3 -> 3; matrix products, arithmetic and copies ran while one was open for 0% -> 0% of each run, Pallas kernels for 25% -> 31%
where the time goes in v2:
time: 75.2 us; the launch traced here: 74.9 us
  Pallas kernels  27.3 us (36%)
  starting transfers between devices  23.5 us (31%)
  waiting for transfers between devices  11.3 us (15%)
  blocking collectives  11.3 us (15%)
    pallas_call x5, Pallas kernels, mass_call(): pl.pallas_call(functools.partial(mass_kernel, jobs, len(arrays), len(smal...  25.7 us
    ppermute x8, starting transfers between devices, move(): return lax.ppermute(value, ('ctx', 'head'), pairs)  23.5 us
    all_to_all x1, blocking collectives, on_device(): spread = lax.all_to_all(local, 'head', 0, 0, tiled=True)  11.3 us
    ppermute x8, waiting for transfers between devices, move(): return lax.ppermute(value, ('ctx', 'head'), pairs)  11.3 us
    pallas_call x1, Pallas kernels, prepare(): pl.pallas_call(prepare_kernel, out_shape=(half,) * 4, in_specs=[pl.BlockS...  1.6 us
  transfers between devices with their start and end apart: 8, of which 3 were waited for; matrix products, arithmetic and copies ran while one was open for 0% of the time, Pallas kernels for 31%

profile of v2, /device:TPU:17, one launch (start us, length us, event | category | flops | bytes accessed | tf_op | source)
XLA Modules:
  0.0 74.9 jit_solution(18067678633252368933)
XLA Ops:
  0.0 0.7 copy-done
  0.7 1.6 %prepare.1 = (bf16[2064,128]{1,0:T(8,128)(2,1)S(1)}, bf16[2064,128]{1,0:T(8,128)(2,1)S(1)}, bf16[2064,128]{1,0:T(8,128)(2,1)S(1)}, bf16[2064,128]{1,0:T(8,128)(2,1)S(1)}) custom-call(bf16[2048,256]{1,0:T(8,128)(2,1)} %q_ref.1, bf16[2048,256]{1,0:T(8,128)(2,1)} %k_ref.1, bf16[2,2048]{1,0:T(2,128)(2,1)S(1)} %copy-done), custom_call_target="tpu_custom_call" | custom-call | tf_op jit(solution)/shard_map/prepare/pallas_call | solution.py:64
  2.3 3.5 %collective-permute-start.1 = (bf16[2064,128]{1,0:T(8,128)(2,1)S(1)}, bf16[2064,128]{1,0:T(8,128)(2,1)S(1)}, u32[]{:S(2)}, u32[]{:S(2)}) collective-permute-start(bf16[2064,128]{1,0:T(8,128)(2,1)S(1)} %get-tuple-element.21.refs_0_), channel_id=1, source_target_pairs={{1,17},{3,19},{5,21},{7,23},{9,25},{11,27},{13,29},{15,31},{16,0},... | collective-permute-start | bytes 1585160 | tf_op jit(solution)/shard_map/ppermute | solution.py:228
  5.9 3.5 %collective-permute-start = (bf16[2064,128]{1,0:T(8,128)(2,1)S(1)}, bf16[2064,128]{1,0:T(8,128)(2,1)S(1)}, u32[]{:S(2)}, u32[]{:S(2)}) collective-permute-start(bf16[2064,128]{1,0:T(8,128)(2,1)S(1)} %get-tuple-element.25.refs_0_), channel_id=1, source_target_pairs={{1,17},{3,19},{5,21},{7,23},{9,25},{11,27},{13,29},{15,31},{16,0},... | collective-permute-start | bytes 1585160 | tf_op jit(solution)/shard_map/ppermute | solution.py:228
  9.4 5.4 %collective-permute-start.4 = (bf16[2064,128]{1,0:T(8,128)(2,1)S(1)}, bf16[2064,128]{1,0:T(8,128)(2,1)S(1)}, u32[]{:S(2)}, u32[]{:S(2)}) collective-permute-start(bf16[2064,128]{1,0:T(8,128)(2,1)S(1)} %get-tuple-element.23.refs_1_), channel_id=1, source_target_pairs={{0,16},{2,18},{4,20},{6,22},{8,24},{10,26},{12,28},{14,30},{16,32}... | collective-permute-start | bytes 1585160 | tf_op jit(solution)/shard_map/ppermute | solution.py:228
  14.8 4.9 %own_a.1.refs_2_ = f32[16,128]{1,0:T(8,128)S(1)} custom-call(bf16[2064,128]{1,0:T(8,128)(2,1)S(1)} %get-tuple-element.21.refs_0_, bf16[2064,128]{1,0:T(8,128)(2,1)S(1)} %get-tuple-element.23.refs_1_, s32[16,128]{1,0:T(8,128)S(1)} %bitcast.4), custom_call_target="tpu_custom_call" | custom-call | flops 1073741824 | bytes 1048576 | tf_op jit(solution)/shard_map/own_a/pallas_call | solution.py:179
  19.7 0.0 collective-permute-done.1.refs_0_.refs_1_
  19.7 4.9 %own_b.1.refs_3_ = f32[16,128]{1,0:T(8,128)S(1)} custom-call(bf16[2064,128]{1,0:T(8,128)(2,1)S(1)} %get-tuple-element.25.refs_0_, bf16[2064,128]{1,0:T(8,128)(2,1)S(1)} %get-tuple-element.28.refs_1_.refs_3_, s32[16,128]{1,0:T(8,128)S(1)} %bitcast.5), custom_call_target="tpu_custom_call" | custom-call | flops 1073741824 | bytes 1048576 | tf_op jit(solution)/shard_map/own_b/pallas_call | solution.py:179
  24.6 2.0 %collective-permute-start.3 = (bf16[2064,128]{1,0:T(8,128)(2,1)S(1)}, bf16[2064,128]{1,0:T(8,128)(2,1)S(1)}, u32[]{:S(2)}, u32[]{:S(2)}) collective-permute-start(bf16[2064,128]{1,0:T(8,128)(2,1)S(1)} %get-tuple-element.28.refs_1_.refs_3_), channel_id=1, source_target_pairs={{0,16},{2,18},{4,20},{6,22},{8,24},{10,26},{12,28},{14,30},{16,32}... | collective-permute-start | bytes 1585160 | tf_op jit(solution)/shard_map/ppermute | solution.py:228
  26.7 3.3 %collective-permute-start.5 = (bf16[2064,128]{1,0:T(8,128)(2,1)S(1)}, bf16[2064,128]{1,0:T(8,128)(2,1)S(1)}, u32[]{:S(2)}, u32[]{:S(2)}) collective-permute-start(bf16[2064,128]{1,0:T(8,128)(2,1)S(1)} %collective-permute-done.1.refs_0_.refs_1_), channel_id=1, source_target_pairs={{1,17},{3,19},{5,21},{7,23},{9,25},{11,27},{13,29},{15,31},{16,0},... | collective-permute-start | bytes 1585160 | tf_op jit(solution)/shard_map/ppermute | solution.py:228
  29.9 0.0 collective-permute-done.refs_2_.refs_3_
  29.9 1.9 %collective-permute-start.2 = (bf16[2064,128]{1,0:T(8,128)(2,1)S(1)}, bf16[2064,128]{1,0:T(8,128)(2,1)S(1)}, u32[]{:S(2)}, u32[]{:S(2)}) collective-permute-start(bf16[2064,128]{1,0:T(8,128)(2,1)S(1)} %collective-permute-done.refs_2_.refs_3_), channel_id=1, source_target_pairs={{1,17},{3,19},{5,21},{7,23},{9,25},{11,27},{13,29},{15,31},{16,0},... | collective-permute-start | bytes 1585160 | tf_op jit(solution)/shard_map/ppermute | solution.py:228
  31.9 0.0 collective-permute-done.4.refs_2_
  31.9 5.4 %first.1.refs_5_.refs_4_ = f32[16,128]{1,0:T(8,128)S(1)} custom-call(bf16[2064,128]{1,0:T(8,128)(2,1)S(1)} %collective-permute-done.1.refs_0_.refs_1_, bf16[2064,128]{1,0:T(8,128)(2,1)S(1)} %get-tuple-element.23.refs_1_, bf16[2064,128]{1,0:T(8,128)(2,1)S(1)} %collective-permute-done.refs_2_.refs_3_, bf16[2064,128]{1,0:T(8,128)(2,1)S(1)} %get-tuple-element.28.refs_1_.refs_3_), custom_call_target="tpu_custom_call" | custom-call | flops 2147483648 | bytes 2097152 | tf_op jit(solution)/shard_map/first/pallas_call | solution.py:179
  37.3 8.8 %collective-permute-done.5.refs_0_ = bf16[2064,128]{1,0:T(8,128)(2,1)S(1)} collective-permute-done((bf16[2064,128]{1,0:T(8,128)(2,1)S(1)}, bf16[2064,128]{1,0:T(8,128)(2,1)S(1)}, u32[]{:S(2)}, u32[]{:S(2)}) %collective-permute-start.5) | collective-permute-done | bytes 528416 | tf_op jit(solution)/shard_map/ppermute | solution.py:228
  46.1 7.8 %middle.1 = (f32[16,128]{1,0:T(8,128)S(1)}, f32[16,128]{1,0:T(8,128)S(1)}, f32[16,128]{1,0:T(8,128)S(1)}) custom-call(bf16[2064,128]{1,0:T(8,128)(2,1)S(1)} %collective-permute-done.5.refs_0_, bf16[2064,128]{1,0:T(8,128)(2,1)S(1)} %collective-permute-done.1.refs_0_.refs_1_, bf16[2064,128]{1,0:T(8,128)(2,1)S(1)} %collective-permute-done.4.refs_2_, ...), custom_call_target="tpu_custom_call" | custom-call | flops 3221225472 | bytes 3145728 | tf_op jit(solution)/shard_map/middle/pallas_call | solution.py:179
  54.0 0.0 collective-permute-done.2.refs_0_
  54.0 2.7 %last.1 = (f32[16,128]{1,0:T(8,128)S(1)}, f32[16,128]{1,0:T(8,128)S(1)}) custom-call(bf16[2064,128]{1,0:T(8,128)(2,1)S(1)} %collective-permute-done.2.refs_0_, bf16[2064,128]{1,0:T(8,128)(2,1)S(1)} %collective-permute-done.3.refs_4_.refs_1_, f32[16,128]{1,0:T(8,128)S(1)} %own_a.1.refs_2_, f32[16,128]{1,0:T(8,128)S(1)} %own_b.1.refs_3_, ...), custom_call_target="tpu_custom_call" | custom-call | flops 1073741824 | bytes 1048576 | tf_op jit(solution)/shard_map/last/pallas_call | solution.py:179
  56.6 1.9 %collective-permute-start.7 = (f32[16,128]{1,0:T(8,128)S(1)}, f32[16,128]{1,0:T(8,128)S(1)}, u32[]{:S(2)}, u32[]{:S(2)}) collective-permute-start(f32[16,128]{1,0:T(8,128)S(1)} %get-tuple-element.34), channel_id=1, source_target_pairs={{16,0},{18,2},{20,4},{22,6},{24,8},{26,10},{28,12},{30,14},{32,16}... | collective-permute-start | bytes 24584 | tf_op jit(solution)/shard_map/ppermute | solution.py:228
  58.6 1.9 %collective-permute-start.6 = (f32[16,128]{1,0:T(8,128)S(1)}, f32[16,128]{1,0:T(8,128)S(1)}, u32[]{:S(2)}, u32[]{:S(2)}) collective-permute-start(f32[16,128]{1,0:T(8,128)S(1)} %get-tuple-element.33), channel_id=1, source_target_pairs={{17,1},{19,3},{21,5},{23,7},{25,9},{27,11},{29,13},{31,15},{33,17}... | collective-permute-start | bytes 24584 | tf_op jit(solution)/shard_map/ppermute | solution.py:228
  60.5 1.4 %collective-permute-done.7 = f32[16,128]{1,0:T(8,128)S(1)} collective-permute-done((f32[16,128]{1,0:T(8,128)S(1)}, f32[16,128]{1,0:T(8,128)S(1)}, u32[]{:S(2)}, u32[]{:S(2)}) %collective-permute-start.7) | collective-permute-done | bytes 8224 | tf_op jit(solution)/shard_map/ppermute | solution.py:228
  61.9 1.0 %collective-permute-done.6 = f32[16,128]{1,0:T(8,128)S(1)} collective-permute-done((f32[16,128]{1,0:T(8,128)S(1)}, f32[16,128]{1,0:T(8,128)S(1)}, u32[]{:S(2)}, u32[]{:S(2)}) %collective-permute-start.6) | collective-permute-done | bytes 8224 | tf_op jit(solution)/shard_map/ppermute | solution.py:228
  63.0 11.3 %all_to_all.9 = f32[16,1,128]{2,1,0:T(1,128)S(1)} all-to-all(f32[16,1,128]{2,1,0:T(1,128)S(1)} %bitcast.6), channel_id=1, replica_groups=mesh['ctx'=16,'head'=16] {'head'}, dimensions={0} | all-to-all | bytes 16384 | tf_op jit(solution)/shard_map/all_to_all | solution.py:273
  74.3 0.5 reduce_sum.9
  (5 shorter events, 0.0 us)
Async XLA Ops:
  0.0 0.7 copy-start
  0.7 14.1 %copy-start.1 = (s32[2048]{0:T(1024)S(1)}, s32[2048]{0:T(1024)}, u32[]{:S(2)}) copy-start(s32[2048]{0:T(1024)} %param.7) | copy-start | bytes 24580
  2.3 17.4 %collective-permute-start.1 = (bf16[2064,128]{1,0:T(8,128)(2,1)S(1)}, bf16[2064,128]{1,0:T(8,128)(2,1)S(1)}, u32[]{:S(2)}, u32[]{:S(2)}) collective-permute-start(bf16[2064,128]{1,0:T(8,128)(2,1)S(1)} %get-tuple-element.21.refs_0_), channel_id=1, source_target_pairs={{1,17},{3,19},{5,21},{7,23},{9,25},{11,27},{13,29},{15,31},{16,0},... | collective-permute-start | bytes 1585160 | tf_op jit(solution)/shard_map/ppermute | solution.py:228
  5.9 24.1 %collective-permute-start = (bf16[2064,128]{1,0:T(8,128)(2,1)S(1)}, bf16[2064,128]{1,0:T(8,128)(2,1)S(1)}, u32[]{:S(2)}, u32[]{:S(2)}) collective-permute-start(bf16[2064,128]{1,0:T(8,128)(2,1)S(1)} %get-tuple-element.25.refs_0_), channel_id=1, source_target_pairs={{1,17},{3,19},{5,21},{7,23},{9,25},{11,27},{13,29},{15,31},{16,0},... | collective-permute-start | bytes 1585160 | tf_op jit(solution)/shard_map/ppermute | solution.py:228
  9.4 22.5 %collective-permute-start.4 = (bf16[2064,128]{1,0:T(8,128)(2,1)S(1)}, bf16[2064,128]{1,0:T(8,128)(2,1)S(1)}, u32[]{:S(2)}, u32[]{:S(2)}) collective-permute-start(bf16[2064,128]{1,0:T(8,128)(2,1)S(1)} %get-tuple-element.23.refs_1_), channel_id=1, source_target_pairs={{0,16},{2,18},{4,20},{6,22},{8,24},{10,26},{12,28},{14,30},{16,32}... | collective-permute-start | bytes 1585160 | tf_op jit(solution)/shard_map/ppermute | solution.py:228
  24.6 12.7 %collective-permute-start.3 = (bf16[2064,128]{1,0:T(8,128)(2,1)S(1)}, bf16[2064,128]{1,0:T(8,128)(2,1)S(1)}, u32[]{:S(2)}, u32[]{:S(2)}) collective-permute-start(bf16[2064,128]{1,0:T(8,128)(2,1)S(1)} %get-tuple-element.28.refs_1_.refs_3_), channel_id=1, source_target_pairs={{0,16},{2,18},{4,20},{6,22},{8,24},{10,26},{12,28},{14,30},{16,32}... | collective-permute-start | bytes 1585160 | tf_op jit(solution)/shard_map/ppermute | solution.py:228
  26.7 19.5 %collective-permute-start.5 = (bf16[2064,128]{1,0:T(8,128)(2,1)S(1)}, bf16[2064,128]{1,0:T(8,128)(2,1)S(1)}, u32[]{:S(2)}, u32[]{:S(2)}) collective-permute-start(bf16[2064,128]{1,0:T(8,128)(2,1)S(1)} %collective-permute-done.1.refs_0_.refs_1_), channel_id=1, source_target_pairs={{1,17},{3,19},{5,21},{7,23},{9,25},{11,27},{13,29},{15,31},{16,0},... | collective-permute-start | bytes 1585160 | tf_op jit(solution)/shard_map/ppermute | solution.py:228
  29.9 24.0 %collective-permute-start.2 = (bf16[2064,128]{1,0:T(8,128)(2,1)S(1)}, bf16[2064,128]{1,0:T(8,128)(2,1)S(1)}, u32[]{:S(2)}, u32[]{:S(2)}) collective-permute-start(bf16[2064,128]{1,0:T(8,128)(2,1)S(1)} %collective-permute-done.refs_2_.refs_3_), channel_id=1, source_target_pairs={{1,17},{3,19},{5,21},{7,23},{9,25},{11,27},{13,29},{15,31},{16,0},... | collective-permute-start | bytes 1585160 | tf_op jit(solution)/shard_map/ppermute | solution.py:228
  56.6 5.3 %collective-permute-start.7 = (f32[16,128]{1,0:T(8,128)S(1)}, f32[16,128]{1,0:T(8,128)S(1)}, u32[]{:S(2)}, u32[]{:S(2)}) collective-permute-start(f32[16,128]{1,0:T(8,128)S(1)} %get-tuple-element.34), channel_id=1, source_target_pairs={{16,0},{18,2},{20,4},{22,6},{24,8},{26,10},{28,12},{30,14},{32,16}... | collective-permute-start | bytes 24584 | tf_op jit(solution)/shard_map/ppermute | solution.py:228
  58.6 4.4 %collective-permute-start.6 = (f32[16,128]{1,0:T(8,128)S(1)}, f32[16,128]{1,0:T(8,128)S(1)}, u32[]{:S(2)}, u32[]{:S(2)}) collective-permute-start(f32[16,128]{1,0:T(8,128)S(1)} %get-tuple-element.33), channel_id=1, source_target_pairs={{17,1},{19,3},{21,5},{23,7},{25,9},{27,11},{29,13},{31,15},{33,17}... | collective-permute-start | bytes 24584 | tf_op jit(solution)/shard_map/ppermute | solution.py:228

commit v3 on v2

v3 whole, which is shorter than its diff:
```python
import functools
import math

import jax
import jax.numpy as jnp
from jax import lax
from jax.experimental import pallas as pl
from jax.experimental.pallas import tpu as pltpu
from jax.sharding import PartitionSpec as P

HD = 128
LANES = 128
LOG2E = math.log2(math.e)
SCORE_SCALE = LOG2E / math.sqrt(HD)
DEAD = 1e30
STEP = 2.0**20
Q_TILE = 256
CONTRACT_LAST = (((1,), (1,)), ((), ()))
VMEM_LIMIT = 40 * 2**20


def role_of_device():
    return lax.rem(lax.axis_index("head"), 2)


def prepare_kernel(q_ref, k_ref, lse_ref, xa_ref, xb_ref, za_ref, zb_ref, wide, lse_rows, sems):
    rows = q_ref.shape[0]
    lse_count = rows // LANES
    role = role_of_device()

    def arrange(moving, fixed):
        lse_in = pltpu.make_async_copy(lse_ref, wide, sems.at[8])
        lse_in.start()
        copies = [
            pltpu.make_async_copy(moving.at[:, :HD], xa_ref.at[:rows], sems.at[0]),
            pltpu.make_async_copy(moving.at[:, HD:], xb_ref.at[:rows], sems.at[1]),
            pltpu.make_async_copy(fixed.at[:, :HD], za_ref.at[:rows], sems.at[2]),
            pltpu.make_async_copy(fixed.at[:, HD:], zb_ref.at[:rows], sems.at[3]),
        ]
        for copy in copies:
            copy.start()
        lse_in.wait()
        lse = wide[...].astype(jnp.float32)
        for head in range(2):
            pieces = [
                lse[head : head + 1, part * LANES : (part + 1) * LANES]
                for part in range(lse_count)
            ]
            lse_rows[head] = jnp.concatenate(pieces, axis=0).astype(jnp.bfloat16)
        for number, (ref, head) in enumerate(
            [(xa_ref, 0), (xb_ref, 1), (za_ref, 0), (zb_ref, 1)]
        ):
            copies.append(
                pltpu.make_async_copy(lse_rows.at[head], ref.at[rows:], sems.at[4 + number])
            )
            copies[-1].start()
        for copy in copies:
            copy.wait()

    pl.when(role == 0)(lambda: arrange(q_ref, k_ref))
    pl.when(role == 1)(lambda: arrange(k_ref, q_ref))


def prepare(key_rows, query_rows, row_lse):
    rows = query_rows.shape[0]
    lse_count = rows // LANES
    half = jax.ShapeDtypeStruct((rows + lse_count, HD), jnp.bfloat16)
    return pl.pallas_call(
        prepare_kernel,
        out_shape=(half,) * 4,
        in_specs=[
            pl.BlockSpec(memory_space=pltpu.HBM),
            pl.BlockSpec(memory_space=pltpu.HBM),
            pl.BlockSpec(memory_space=pltpu.HBM),
        ],
        out_specs=(pl.BlockSpec(memory_space=pl.ANY),) * 4,
        scratch_shapes=[
            pltpu.VMEM(row_lse.shape, jnp.bfloat16),
            pltpu.VMEM((2, lse_count, LANES), jnp.bfloat16),
            pltpu.SemaphoreType.DMA((9,)),
        ],
        compiler_params=pltpu.CompilerParams(vmem_limit_bytes=VMEM_LIMIT),
        name="prepare",
    )(
        pltpu.with_memory_space_constraint(query_rows, pltpu.HBM),
        pltpu.with_memory_space_constraint(key_rows, pltpu.HBM),
        pltpu.with_memory_space_constraint(row_lse, pltpu.HBM),
    )


def add_pair(q_buf, k_buf, lse_buf, offsets, key_steps, acc, is_first, is_live):
    lse = lse_buf[...].astype(jnp.float32) * LOG2E
    lse = jnp.where(is_live, lse, DEAD)
    parts = Q_TILE // LANES
    for tile in range(q_buf.shape[0] // Q_TILE):
        scores = lax.dot_general(
            k_buf[...],
            q_buf[tile * Q_TILE : (tile + 1) * Q_TILE, :],
            CONTRACT_LAST,
            preferred_element_type=jnp.float32,
        )
        total = None
        for part in range(parts):
            row = tile * parts + part
            exponent = (
                scores[:, part * LANES : (part + 1) * LANES] * SCORE_SCALE - lse[row : row + 1, :]
            )
            if offsets is not None:
                ceiling = offsets[row : row + 1, :] - key_steps[...]
                exponent = jnp.minimum(exponent, ceiling)
            weights = jnp.exp2(exponent)
            total = weights if total is None else total + weights
        if is_first and tile == 0:
            acc[...] = total
        else:
            acc[...] += total


def turned_mass(acc, count):
    parts = []
    for part in range(count):
        turned = acc[part * LANES : (part + 1) * LANES, :].T
        parts.append(jnp.sum(turned, axis=0, keepdims=True))
    return jnp.concatenate(parts, axis=0)


def mass_kernel(jobs, n_arrays, n_small, finish, is_own, *refs):
    arrays = refs[:n_arrays]
    small = refs[n_arrays : n_arrays + n_small]
    outs = refs[n_arrays + n_small : n_arrays + n_small + 1]
    q_buf, k_buf, lse_buf, acc, key_steps, sems = refs[n_arrays + n_small + 1 :]
    rows = q_buf.shape[1]
    lse_count = lse_buf.shape[1]
    role = role_of_device()
    shard = lax.axis_index("ctx")
    shards = lax.axis_size("ctx")

    def copies_of(number, chosen):
        query, key, _ = jobs[number][chosen]
        return [
            pltpu.make_async_copy(arrays[key].at[:rows], k_buf.at[number], sems.at[number, 0]),
            pltpu.make_async_copy(arrays[query].at[:rows], q_buf.at[number], sems.at[number, 1]),
            pltpu.make_async_copy(arrays[query].at[rows:], lse_buf.at[number], sems.at[number, 2]),
        ]

    def start_all(chosen):
        for number in range(len(jobs)):
            for copy in copies_of(number, chosen):
                copy.start()

    pl.when(role == 0)(lambda: start_all(0))
    pl.when(role == 1)(lambda: start_all(1))
    if is_own:
        first_rows = lax.broadcasted_iota(jnp.int32, (64, LANES), 0).astype(jnp.float32) * STEP

        def fill(number, carry):
            start = pl.multiple_of(number * 64, 64)
            key_steps[pl.ds(start, 64), :] = first_rows + start.astype(jnp.float32) * STEP
            return carry

        lax.fori_loop(0, rows // 64, fill, 0)
    for number, job in enumerate(jobs):
        for copy in copies_of(number, 0):
            copy.wait()
        add_pair(
            q_buf.at[number],
            k_buf.at[number],
            lse_buf.at[number],
            (small[0][...].astype(jnp.float32) + 0.5) * STEP if is_own else None,
            key_steps,
            acc,
            number == 0,
            shard + jnp.where(role == 0, job[0][2], job[1][2]) < shards,
        )
    mass = turned_mass(acc, lse_count)
    outs[0][...] = mass if finish is None else finish(role, mass, [ref[...] for ref in small])


def mass_call(name, arrays, jobs, small=(), finish=None, is_own=False):
    padded = arrays[0].shape[0]
    rows = padded * LANES // (LANES + 1)
    lse_count = padded - rows
    pairs = len(jobs) * rows * rows
    return pl.pallas_call(
        functools.partial(mass_kernel, jobs, len(arrays), len(small), finish, is_own),
        out_shape=jax.ShapeDtypeStruct((lse_count, LANES), jnp.float32),
        in_specs=[pl.BlockSpec(memory_space=pl.ANY)] * len(arrays)
        + [pl.BlockSpec(memory_space=pltpu.VMEM)] * len(small),
        out_specs=pl.BlockSpec(memory_space=pltpu.VMEM),
        scratch_shapes=[
            pltpu.VMEM((len(jobs), rows, HD), jnp.bfloat16),
            pltpu.VMEM((len(jobs), rows, HD), jnp.bfloat16),
            pltpu.VMEM((len(jobs), lse_count, LANES), jnp.bfloat16),
            pltpu.VMEM((rows, LANES), jnp.float32),
            pltpu.VMEM((rows if is_own else 8, LANES), jnp.float32),
            pltpu.SemaphoreType.DMA((len(jobs), 3)),
        ],
        compiler_params=pltpu.CompilerParams(vmem_limit_bytes=VMEM_LIMIT),
        cost_estimate=pl.CostEstimate(
            flops=2 * pairs * HD, transcendentals=pairs, bytes_accessed=len(jobs) * 2**20
        ),
        name=name,
    )(*arrays, *small)


def job(core_0, core_1):
    return (core_0, core_1)


def finish_last(role, mass, small):
    last_a, middle_a, middle_b = small
    return mass + last_a + jnp.where(role == 1, middle_a + middle_b, 0.0)


def finish_first(role, mass, small):
    own_a, own_b, middle_a, middle_b, first_a = small
    return mass + own_a + own_b + first_a + jnp.where(role == 0, middle_a + middle_b, 0.0)


def move(value, mesh_shape, steps_of_role):
    shards, heads = mesh_shape
    pairs = []
    for shard in range(shards):
        for head in range(heads):
            steps = steps_of_role[head % 2]
            if steps != 0 and 0 <= shard + steps < shards:
                pairs.append((shard * heads + head, (shard + steps) * heads + head))
    return lax.ppermute(value, ("ctx", "head"), pairs)


def after(value, *done):
    return lax.optimization_barrier((value, *done))[0]


def on_device(mesh_shape, key_rows, query_rows, row_lse, query_offsets):
    rows = query_rows.shape[0]
    out, back = (-1, 1), (1, -1)
    xa0, xb0, za0, zb0 = prepare(key_rows, query_rows, row_lse)
    offsets = query_offsets.reshape(rows // LANES, LANES)
    own = [job((0, 1, 0), (1, 0, 0))]
    middle = [job((0, 1, 2), (1, 0, 0))]
    last = [job((0, 1, 2), (1, 0, 1))]
    first = [job((0, 1, 1), (2, 3, 1))]

    xa1 = move(xa0, mesh_shape, out)
    xb1 = move(xb0, mesh_shape, out)
    za1 = move(za0, mesh_shape, back)
    own_a = mass_call("own_a", [xa0, za0], own, (offsets,), is_own=True)
    xa1 = after(xa1, own_a)
    xa2 = move(xa1, mesh_shape, out)
    own_b = mass_call("own_b", [after(xb0, xa1), zb0], own, (offsets,), is_own=True)
    xb1 = after(xb1, own_b)
    xb2 = move(xb1, mesh_shape, out)
    zb1 = move(after(zb0, xb1), mesh_shape, back)
    first_a = mass_call("first_a", [after(xa1, xb1), za0, za1, xa0], first)
    middle_a = mass_call("middle_a", [after(xa2, first_a), za0], middle)
    last_a = mass_call("last_a", [after(xa2, middle_a), za1], last)
    middle_b = mass_call("middle_b", [xb2, after(zb0, last_a)], middle)
    far = mass_call(
        "last_b",
        [xb2, after(zb1, middle_b)],
        last,
        (last_a, middle_a, middle_b),
        finish=finish_last,
    )
    local = mass_call(
        "first_b",
        [after(xb1, far), zb0, zb1, xb0],
        first,
        (own_a, own_b, middle_a, middle_b, first_a),
        finish=finish_first,
    )
    local = local + move(far, mesh_shape, (-1, -2))
    spread = lax.all_to_all(local, "head", 0, 0, tiled=True)
    return jnp.sum(spread, axis=0)


def solution(mesh):
    mesh_shape = (mesh.shape["ctx"], mesh.shape["head"])
    in_specs = (P("ctx", "head"), P("ctx", "head"), P("head", "ctx"), P("ctx"))
    out_specs = P(("ctx", "head"))
    return jax.shard_map(
        functools.partial(on_device, mesh_shape),
        mesh=mesh,
        in_specs=in_specs,
        out_specs=out_specs,
        check_vma=False,
    )
```

time: 75.2 us -> 73.9 us (0.983)
  waiting for transfers between devices: 11.3 us -> 0.02 us
  blocking collectives: 11.3 us -> 19.5 us
  starting transfers between devices: 23.5 us -> 27.7 us
  Pallas kernels: 27.3 us -> 25.6 us
    ppermute x8 -> x7, waiting for transfers between devices: 11.3 us -> 0.02 us  [move(): return lax.ppermute(value, ('ctx', 'head'), pairs)]
    all_to_all x1, blocking collectives: 11.3 us -> 19.5 us  [on_device(): spread = lax.all_to_all(local, 'head', 0, 0, tiled=True)]
    ppermute x8 -> x7, starting transfers between devices: 23.5 us -> 27.7 us  [move(): return lax.ppermute(value, ('ctx', 'head'), pairs)]
    pallas_call x5 -> x8, Pallas kernels: 25.7 us -> 24 us  [mass_call(): pl.pallas_call(functools.partial(mass_kernel, jobs, len(arrays), len(smal...]
  transfers between devices with their start and end apart: 8 -> 7, of which waited for: 3 -> 0; matrix products, arithmetic and copies ran while one was open for 0% -> 0% of each run, Pallas kernels for 31% -> 29%
where the time goes in v3:
time: 73.9 us; the launch traced here: 73.6 us
  starting transfers between devices  27.7 us (37%)
  Pallas kernels  25.6 us (35%)
  blocking collectives  19.5 us (26%)
    ppermute x7, starting transfers between devices, move(): return lax.ppermute(value, ('ctx', 'head'), pairs)  27.7 us
    pallas_call x8, Pallas kernels, mass_call(): pl.pallas_call(functools.partial(mass_kernel, jobs, len(arrays), len(smal...  24 us
    all_to_all x1, blocking collectives, on_device(): spread = lax.all_to_all(local, 'head', 0, 0, tiled=True)  19.5 us
    pallas_call x1, Pallas kernels, prepare(): pl.pallas_call(prepare_kernel, out_shape=(half,) * 4, in_specs=[pl.BlockS...  1.63 us
  transfers between devices with their start and end apart: 7, of which 0 were waited for; matrix products, arithmetic and copies ran while one was open for 0% of the time, Pallas kernels for 29%

profile of v3, /device:TPU:17, one launch (start us, length us, event | category | flops | bytes accessed | tf_op | source)
XLA Modules:
  0.0 73.6 jit_solution(11283966337097945946)
XLA Ops:
  0.0 1.6 %prepare.1 = (bf16[2064,128]{1,0:T(8,128)(2,1)S(1)}, bf16[2064,128]{1,0:T(8,128)(2,1)S(1)}, bf16[2064,128]{1,0:T(8,128)(2,1)S(1)}, bf16[2064,128]{1,0:T(8,128)(2,1)S(1)}) custom-call(bf16[2048,256]{1,0:T(8,128)(2,1)} %q_ref.1, bf16[2048,256]{1,0:T(8,128)(2,1)} %k_ref.1, bf16[2,2048]{1,0:T(2,128)(2,1)} %lse_ref.1), custom_call_target="tpu_custom_call" | custom-call | tf_op jit(solution)/shard_map/prepare/pallas_call | solution.py:68
  1.6 3.5 %collective-permute-start.1 = (bf16[2064,128]{1,0:T(8,128)(2,1)S(1)}, bf16[2064,128]{1,0:T(8,128)(2,1)S(1)}, u32[]{:S(2)}, u32[]{:S(2)}) collective-permute-start(bf16[2064,128]{1,0:T(8,128)(2,1)S(1)} %get-tuple-element.20.refs_0_.refs_3_), channel_id=1, source_target_pairs={{1,17},{3,19},{5,21},{7,23},{9,25},{11,27},{13,29},{15,31},{16,0},... | collective-permute-start | bytes 1585160 | tf_op jit(solution)/shard_map/ppermute | solution.py:228
  5.2 3.5 %collective-permute-start = (bf16[2064,128]{1,0:T(8,128)(2,1)S(1)}, bf16[2064,128]{1,0:T(8,128)(2,1)S(1)}, u32[]{:S(2)}, u32[]{:S(2)}) collective-permute-start(bf16[2064,128]{1,0:T(8,128)(2,1)S(1)} %get-tuple-element.23.refs_0_.refs_3_), channel_id=1, source_target_pairs={{1,17},{3,19},{5,21},{7,23},{9,25},{11,27},{13,29},{15,31},{16,0},... | collective-permute-start | bytes 1585160 | tf_op jit(solution)/shard_map/ppermute | solution.py:228
  8.7 5.4 %collective-permute-start.5 = (bf16[2064,128]{1,0:T(8,128)(2,1)S(1)}, bf16[2064,128]{1,0:T(8,128)(2,1)S(1)}, u32[]{:S(2)}, u32[]{:S(2)}) collective-permute-start(bf16[2064,128]{1,0:T(8,128)(2,1)S(1)} %get-tuple-element.21.refs_1_), channel_id=1, source_target_pairs={{0,16},{2,18},{4,20},{6,22},{8,24},{10,26},{12,28},{14,30},{16,32}... | collective-permute-start | bytes 1585160 | tf_op jit(solution)/shard_map/ppermute | solution.py:228
  14.1 3.8 %own_a.1.refs_4_ = f32[16,128]{1,0:T(8,128)S(1)} custom-call(bf16[2064,128]{1,0:T(8,128)(2,1)S(1)} %get-tuple-element.20.refs_0_.refs_3_, bf16[2064,128]{1,0:T(8,128)(2,1)S(1)} %get-tuple-element.21.refs_1_, s32[16,128]{1,0:T(8,128)S(1)} %bitcast.4), custom_call_target="tpu_custom_call" | custom-call | flops 1073741824 | bytes 1048576 | tf_op jit(solution)/shard_map/own_a/pallas_call | solution.py:184
  17.9 0.0 collective-permute-done.1.refs_0_
  18.0 1.9 %collective-permute-start.4 = (bf16[2064,128]{1,0:T(8,128)(2,1)S(1)}, bf16[2064,128]{1,0:T(8,128)(2,1)S(1)}, u32[]{:S(2)}, u32[]{:S(2)}) collective-permute-start(bf16[2064,128]{1,0:T(8,128)(2,1)S(1)} %collective-permute-done.1.refs_0_), channel_id=1, source_target_pairs={{1,17},{3,19},{5,21},{7,23},{9,25},{11,27},{13,29},{15,31},{16,0},... | collective-permute-start | bytes 1585160 | tf_op jit(solution)/shard_map/ppermute | solution.py:228
  19.9 3.8 %own_b.1.refs_5_ = f32[16,128]{1,0:T(8,128)S(1)} custom-call(bf16[2064,128]{1,0:T(8,128)(2,1)S(1)} %get-tuple-element.23.refs_0_.refs_3_, bf16[2064,128]{1,0:T(8,128)(2,1)S(1)} %get-tuple-element.30.refs_1_, s32[16,128]{1,0:T(8,128)S(1)} %bitcast.5), custom_call_target="tpu_custom_call" | custom-call | flops 1073741824 | bytes 1048576 | tf_op jit(solution)/shard_map/own_b/pallas_call | solution.py:184
  23.7 0.0 collective-permute-done.refs_0_
  23.7 3.0 %collective-permute-start.2 = (bf16[2064,128]{1,0:T(8,128)(2,1)S(1)}, bf16[2064,128]{1,0:T(8,128)(2,1)S(1)}, u32[]{:S(2)}, u32[]{:S(2)}) collective-permute-start(bf16[2064,128]{1,0:T(8,128)(2,1)S(1)} %collective-permute-done.refs_0_), channel_id=1, source_target_pairs={{1,17},{3,19},{5,21},{7,23},{9,25},{11,27},{13,29},{15,31},{16,0},... | collective-permute-start | bytes 1585160 | tf_op jit(solution)/shard_map/ppermute | solution.py:228
  26.7 5.9 %collective-permute-start.3 = (bf16[2064,128]{1,0:T(8,128)(2,1)S(1)}, bf16[2064,128]{1,0:T(8,128)(2,1)S(1)}, u32[]{:S(2)}, u32[]{:S(2)}) collective-permute-start(bf16[2064,128]{1,0:T(8,128)(2,1)S(1)} %get-tuple-element.30.refs_1_), channel_id=1, source_target_pairs={{0,16},{2,18},{4,20},{6,22},{8,24},{10,26},{12,28},{14,30},{16,32}... | collective-permute-start | bytes 1585160 | tf_op jit(solution)/shard_map/ppermute | solution.py:228
  32.6 0.0 collective-permute-done.5.refs_2_.refs_1_
  32.7 2.7 %first_a.1.refs_8_ = f32[16,128]{1,0:T(8,128)S(1)} custom-call(bf16[2064,128]{1,0:T(8,128)(2,1)S(1)} %collective-permute-done.1.refs_0_, bf16[2064,128]{1,0:T(8,128)(2,1)S(1)} %get-tuple-element.21.refs_1_, bf16[2064,128]{1,0:T(8,128)(2,1)S(1)} %collective-permute-done.5.refs_2_.refs_1_, bf16[2064,128]{1,0:T(8,128)(2,1)S(1)} %get-tuple-element.20.refs_0_.refs_3_), custom_call_target="tpu_custom_call" | custom-call | flops 1073741824 | bytes 1048576 | tf_op jit(solution)/shard_map/first_a/pallas_call | solution.py:184
  35.3 0.0 collective-permute-done.4.refs_0_
  35.3 2.8 %middle_a.1.refs_3_.refs_6_ = f32[16,128]{1,0:T(8,128)S(1)} custom-call(bf16[2064,128]{1,0:T(8,128)(2,1)S(1)} %collective-permute-done.4.refs_0_, bf16[2064,128]{1,0:T(8,128)(2,1)S(1)} %get-tuple-element.21.refs_1_), custom_call_target="tpu_custom_call" | custom-call | flops 1073741824 | bytes 1048576 | tf_op jit(solution)/shard_map/middle_a/pallas_call | solution.py:184
  38.2 2.7 %last_a.1.refs_2_ = f32[16,128]{1,0:T(8,128)S(1)} custom-call(bf16[2064,128]{1,0:T(8,128)(2,1)S(1)} %collective-permute-done.4.refs_0_, bf16[2064,128]{1,0:T(8,128)(2,1)S(1)} %collective-permute-done.5.refs_2_.refs_1_), custom_call_target="tpu_custom_call" | custom-call | flops 1073741824 | bytes 1048576 | tf_op jit(solution)/shard_map/last_a/pallas_call | solution.py:184
  40.8 0.0 collective-permute-done.2.refs_0_
  40.8 2.7 %middle_b.1.refs_4_.refs_7_ = f32[16,128]{1,0:T(8,128)S(1)} custom-call(bf16[2064,128]{1,0:T(8,128)(2,1)S(1)} %collective-permute-done.2.refs_0_, bf16[2064,128]{1,0:T(8,128)(2,1)S(1)} %get-tuple-element.30.refs_1_), custom_call_target="tpu_custom_call" | custom-call | flops 1073741824 | bytes 1048576 | tf_op jit(solution)/shard_map/middle_b/pallas_call | solution.py:184
  43.5 0.0 collective-permute-done.3.refs_1_.refs_2_
  43.5 2.7 %last_b.1 = f32[16,128]{1,0:T(8,128)S(1)} custom-call(bf16[2064,128]{1,0:T(8,128)(2,1)S(1)} %collective-permute-done.2.refs_0_, bf16[2064,128]{1,0:T(8,128)(2,1)S(1)} %collective-permute-done.3.refs_1_.refs_2_, f32[16,128]{1,0:T(8,128)S(1)} %last_a.1.refs_2_, f32[16,128]{1,0:T(8,128)S(1)} %middle_a.1.refs_3_.refs_6_, f32[16,128]{1,0:T(8,128)S(1)} %middle_b.1.refs_4_.refs_7_), custom_call_target="tpu_custom_call" | custom-call | flops 1073741824 | bytes 1048576 | tf_op jit(solution)/shard_map/last_b/pallas_call | solution.py:184
  46.2 4.4 %collective-permute-start.6 = (f32[16,128]{1,0:T(8,128)S(1)}, f32[16,128]{1,0:T(8,128)S(1)}, u32[]{:S(2)}, u32[]{:S(2)}) collective-permute-start(f32[16,128]{1,0:T(8,128)S(1)} %last_b.1), channel_id=1, source_target_pairs={{16,0},{18,2},{20,4},{22,6},{24,8},{26,10},{28,12},{30,14},{32,16}... | collective-permute-start | bytes 24584 | tf_op jit(solution)/shard_map/ppermute | solution.py:228
  50.6 2.9 %first_b.1 = f32[16,128]{1,0:T(8,128)S(1)} custom-call(bf16[2064,128]{1,0:T(8,128)(2,1)S(1)} %collective-permute-done.refs_0_, bf16[2064,128]{1,0:T(8,128)(2,1)S(1)} %get-tuple-element.30.refs_1_, bf16[2064,128]{1,0:T(8,128)(2,1)S(1)} %collective-permute-done.3.refs_1_.refs_2_, bf16[2064,128]{1,0:T(8,128)(2,1)S(1)} %get-tuple-element.23.refs_0_.refs_3_, ...), custom_call_target="tpu_custom_call" | custom-call | flops 1073741824 | bytes 1048576 | tf_op jit(solution)/shard_map/first_b/pallas_call | solution.py:184
  53.5 19.5 %all_to_all.9 = f32[16,1,128]{2,1,0:T(1,128)S(1)} all-to-all(f32[16,1,128]{2,1,0:T(1,128)S(1)} %bitcast.6), channel_id=1, replica_groups=mesh['ctx'=16,'head'=16] {'head'}, dimensions={0} | all-to-all | bytes 16384 | tf_op jit(solution)/shard_map/all_to_all | solution.py:274
  73.0 0.5 reduce_sum.9
  (4 shorter events, 0.0 us)
Async XLA Ops:
  0.0 14.1 %copy-start = (s32[2048]{0:T(1024)S(1)}, s32[2048]{0:T(1024)}, u32[]{:S(2)}) copy-start(s32[2048]{0:T(1024)} %param.7) | copy-start | bytes 24580
  1.6 16.3 %collective-permute-start.1 = (bf16[2064,128]{1,0:T(8,128)(2,1)S(1)}, bf16[2064,128]{1,0:T(8,128)(2,1)S(1)}, u32[]{:S(2)}, u32[]{:S(2)}) collective-permute-start(bf16[2064,128]{1,0:T(8,128)(2,1)S(1)} %get-tuple-element.20.refs_0_.refs_3_), channel_id=1, source_target_pairs={{1,17},{3,19},{5,21},{7,23},{9,25},{11,27},{13,29},{15,31},{16,0},... | collective-permute-start | bytes 1585160 | tf_op jit(solution)/shard_map/ppermute | solution.py:228
  5.2 18.5 %collective-permute-start = (bf16[2064,128]{1,0:T(8,128)(2,1)S(1)}, bf16[2064,128]{1,0:T(8,128)(2,1)S(1)}, u32[]{:S(2)}, u32[]{:S(2)}) collective-permute-start(bf16[2064,128]{1,0:T(8,128)(2,1)S(1)} %get-tuple-element.23.refs_0_.refs_3_), channel_id=1, source_target_pairs={{1,17},{3,19},{5,21},{7,23},{9,25},{11,27},{13,29},{15,31},{16,0},... | collective-permute-start | bytes 1585160 | tf_op jit(solution)/shard_map/ppermute | solution.py:228
  8.7 23.9 %collective-permute-start.5 = (bf16[2064,128]{1,0:T(8,128)(2,1)S(1)}, bf16[2064,128]{1,0:T(8,128)(2,1)S(1)}, u32[]{:S(2)}, u32[]{:S(2)}) collective-permute-start(bf16[2064,128]{1,0:T(8,128)(2,1)S(1)} %get-tuple-element.21.refs_1_), channel_id=1, source_target_pairs={{0,16},{2,18},{4,20},{6,22},{8,24},{10,26},{12,28},{14,30},{16,32}... | collective-permute-start | bytes 1585160 | tf_op jit(solution)/shard_map/ppermute | solution.py:228
  18.0 17.4 %collective-permute-start.4 = (bf16[2064,128]{1,0:T(8,128)(2,1)S(1)}, bf16[2064,128]{1,0:T(8,128)(2,1)S(1)}, u32[]{:S(2)}, u32[]{:S(2)}) collective-permute-start(bf16[2064,128]{1,0:T(8,128)(2,1)S(1)} %collective-permute-done.1.refs_0_), channel_id=1, source_target_pairs={{1,17},{3,19},{5,21},{7,23},{9,25},{11,27},{13,29},{15,31},{16,0},... | collective-permute-start | bytes 1585160 | tf_op jit(solution)/shard_map/ppermute | solution.py:228
  23.7 17.1 %collective-permute-start.2 = (bf16[2064,128]{1,0:T(8,128)(2,1)S(1)}, bf16[2064,128]{1,0:T(8,128)(2,1)S(1)}, u32[]{:S(2)}, u32[]{:S(2)}) collective-permute-start(bf16[2064,128]{1,0:T(8,128)(2,1)S(1)} %collective-permute-done.refs_0_), channel_id=1, source_target_pairs={{1,17},{3,19},{5,21},{7,23},{9,25},{11,27},{13,29},{15,31},{16,0},... | collective-permute-start | bytes 1585160 | tf_op jit(solution)/shard_map/ppermute | solution.py:228
  26.7 16.8 %collective-permute-start.3 = (bf16[2064,128]{1,0:T(8,128)(2,1)S(1)}, bf16[2064,128]{1,0:T(8,128)(2,1)S(1)}, u32[]{:S(2)}, u32[]{:S(2)}) collective-permute-start(bf16[2064,128]{1,0:T(8,128)(2,1)S(1)} %get-tuple-element.30.refs_1_), channel_id=1, source_target_pairs={{0,16},{2,18},{4,20},{6,22},{8,24},{10,26},{12,28},{14,30},{16,32}... | collective-permute-start | bytes 1585160 | tf_op jit(solution)/shard_map/ppermute | solution.py:228
  46.2 7.3 %collective-permute-start.6 = (f32[16,128]{1,0:T(8,128)S(1)}, f32[16,128]{1,0:T(8,128)S(1)}, u32[]{:S(2)}, u32[]{:S(2)}) collective-permute-start(f32[16,128]{1,0:T(8,128)S(1)} %last_b.1), channel_id=1, source_target_pairs={{16,0},{18,2},{20,4},{22,6},{24,8},{26,10},{28,12},{30,14},{32,16}... | collective-permute-start | bytes 24584 | tf_op jit(solution)/shard_map/ppermute | solution.py:228

commit v4 on v3

--- a/solution.py
+++ b/solution.py
@@ -135,6 +135,8 @@
     shard = lax.axis_index("ctx")
     shards = lax.axis_size("ctx")
 
+    upper = shard >= shards // 2
+
     def copies_of(number, chosen):
         query, key, _ = jobs[number][chosen]
         return [
@@ -143,13 +145,15 @@
             pltpu.make_async_copy(arrays[query].at[rows:], lse_buf.at[number], sems.at[number, 2]),
         ]
 
-    def start_all(chosen):
-        for number in range(len(jobs)):
-            for copy in copies_of(number, chosen):
-                copy.start()
-
-    pl.when(role == 0)(lambda: start_all(0))
-    pl.when(role == 1)(lambda: start_all(1))
+    def start_job(number, chosen):
+        for copy in copies_of(number, chosen):
+            copy.start()
+
+    for number, (_, _, gate) in enumerate(jobs):
+        wanted = True if gate is None else gate(role, upper)
+        for chosen in range(2):
+            if jobs[number][chosen] is not None:
+                pl.when((role == chosen) & wanted)(functools.partial(start_job, number, chosen))
     if is_own:
         first_rows = lax.broadcasted_iota(jnp.int32, (64, LANES), 0).astype(jnp.float32) * STEP
 
@@ -159,9 +163,11 @@
             return carry
 
         lax.fori_loop(0, rows // 64, fill, 0)
-    for number, job in enumerate(jobs):
-        for copy in copies_of(number, 0):
+    def run(number):
+        chosen = 0 if jobs[number][0] is not None else 1
+        for copy in copies_of(number, chosen):
             copy.wait()
+        steps = [0 if entry is None else entry[2] for entry in jobs[number][:2]]
         add_pair(
             q_buf.at[number],
             k_buf.at[number],
@@ -170,8 +176,21 @@
             key_steps,
             acc,
             number == 0,
-            shard + jnp.where(role == 0, job[0][2], job[1][2]) < shards,
+            shard + jnp.where(role == 0, steps[0], steps[1]) < shards,
         )
+
+    for number, (_, _, gate) in enumerate(jobs):
+        if gate is None:
+            run(number)
+            continue
+        wanted = gate(role, upper)
+        if number == 0:
+
+            @pl.when(jnp.logical_not(wanted))
+            def _():
+                acc[...] = jnp.zeros_like(acc)
+
+        pl.when(wanted)(functools.partial(run, number))
     mass = turned_mass(acc, lse_count)
     outs[0][...] = mass if finish is None else finish(role, mass, [ref[...] for ref in small])
 
@@ -203,17 +222,25 @@
     )(*arrays, *small)
 
 
-def job(core_0, core_1):
-    return (core_0, core_1)
-
-
-def finish_last(role, mass, small):
+def job(core_0, core_1, gate=None):
+    return (core_0, core_1, gate)
+
+
+def runs_early(role, upper):
+    return (role == 1) | upper
+
+
+def runs_late(role, upper):
+    return (role == 0) & jnp.logical_not(upper)
+
+
+def finish_far(role, mass, small):
     last_a, middle_a, middle_b = small
     return mass + last_a + jnp.where(role == 1, middle_a + middle_b, 0.0)
 
 
-def finish_first(role, mass, small):
-    own_a, own_b, middle_a, middle_b, first_a = small
+def finish_near(role, mass, small):
+    own_a, own_b, first_a, middle_a, middle_b = small
     return mass + own_a + own_b + first_a + jnp.where(role == 0, middle_a + middle_b, 0.0)
 
 
@@ -240,7 +267,9 @@
     own = [job((0, 1, 0), (1, 0, 0))]
     middle = [job((0, 1, 2), (1, 0, 0))]
     last = [job((0, 1, 2), (1, 0, 1))]
+    middle_early = [job((0, 1, 2), (1, 0, 0), runs_early)]
     first = [job((0, 1, 1), (2, 3, 1))]
+    near_jobs = [job((0, 1, 1), (2, 3, 1)), job((4, 1, 2), None, runs_late)]
 
     xa1 = move(xa0, mesh_shape, out)
     xb1 = move(xb0, mesh_shape, out)
@@ -251,24 +280,24 @@
     own_b = mass_call("own_b", [after(xb0, xa1), zb0], own, (offsets,), is_own=True)
     xb1 = after(xb1, own_b)
     xb2 = move(xb1, mesh_shape, out)
-    zb1 = move(after(zb0, xb1), mesh_shape, back)
-    first_a = mass_call("first_a", [after(xa1, xb1), za0, za1, xa0], first)
-    middle_a = mass_call("middle_a", [after(xa2, first_a), za0], middle)
+    zb1 = move(after(zb0, xb1, za1), mesh_shape, back)
+    middle_a = mass_call("middle_a", [after(xa2, xb1, za1), za0], middle)
     last_a = mass_call("last_a", [after(xa2, middle_a), za1], last)
-    middle_b = mass_call("middle_b", [xb2, after(zb0, last_a)], middle)
+    first_a = mass_call("first_a", [after(xa1, last_a), za0, za1, xa0], first)
+    middle_b = mass_call("middle_b", [xb2, after(zb0, first_a)], middle_early)
     far = mass_call(
         "last_b",
         [xb2, after(zb1, middle_b)],
         last,
         (last_a, middle_a, middle_b),
-        finish=finish_last,
+        finish=finish_far,
     )
     local = mass_call(
-        "first_b",
-        [after(xb1, far), zb0, zb1, xb0],
-        first,
-        (own_a, own_b, middle_a, middle_b, first_a),
-        finish=finish_first,
+        "near",
+        [after(xb1, far), zb0, zb1, xb0, xb2],
+        near_jobs,
+        (own_a, own_b, first_a, middle_a, middle_b),
+        finish=finish_near,
     )
     local = local + move(far, mesh_shape, (-1, -2))
     spread = lax.all_to_all(local, "head", 0, 0, tiled=True)

time: 73.9 us -> 71.9 us (0.973)
  blocking collectives: 19.5 us -> 17.3 us
    all_to_all x1, blocking collectives: 19.5 us -> 17.3 us  [on_device(): spread = lax.all_to_all(local, 'head', 0, 0, tiled=True)]
  transfers between devices with their start and end apart: 7 -> 7, of which waited for: 0 -> 0; matrix products, arithmetic and copies ran while one was open for 0% -> 0% of each run, Pallas kernels for 29% -> 30%
where the time goes in v4:
time: 71.9 us; the launch traced here: 71.6 us
  starting transfers between devices  27.5 us (38%)
  Pallas kernels  26 us (36%)
  blocking collectives  17.3 us (24%)
    ppermute x7, starting transfers between devices, move(): return lax.ppermute(value, ('ctx', 'head'), pairs)  27.5 us
    pallas_call x8, Pallas kernels, mass_call(): pl.pallas_call(functools.partial(mass_kernel, jobs, len(arrays), len(smal...  24.4 us
    all_to_all x1, blocking collectives, on_device(): spread = lax.all_to_all(local, 'head', 0, 0, tiled=True)  17.3 us
    pallas_call x1, Pallas kernels, prepare(): pl.pallas_call(prepare_kernel, out_shape=(half,) * 4, in_specs=[pl.BlockS...  1.63 us
  transfers between devices with their start and end apart: 7, of which 0 were waited for; matrix products, arithmetic and copies ran while one was open for 0% of the time, Pallas kernels for 30%

profile of v4, /device:TPU:17, one launch (start us, length us, event | category | flops | bytes accessed | tf_op | source)
XLA Modules:
  0.0 71.6 jit_solution(7307033318297906906)
XLA Ops:
  0.0 1.6 %prepare.1 = (bf16[2064,128]{1,0:T(8,128)(2,1)S(1)}, bf16[2064,128]{1,0:T(8,128)(2,1)S(1)}, bf16[2064,128]{1,0:T(8,128)(2,1)S(1)}, bf16[2064,128]{1,0:T(8,128)(2,1)S(1)}) custom-call(bf16[2048,256]{1,0:T(8,128)(2,1)} %q_ref.1, bf16[2048,256]{1,0:T(8,128)(2,1)} %k_ref.1, bf16[2,2048]{1,0:T(2,128)(2,1)} %lse_ref.1), custom_call_target="tpu_custom_call" | custom-call | tf_op jit(solution)/shard_map/prepare/pallas_call | solution.py:68
  1.6 3.5 %collective-permute-start.1 = (bf16[2064,128]{1,0:T(8,128)(2,1)S(1)}, bf16[2064,128]{1,0:T(8,128)(2,1)S(1)}, u32[]{:S(2)}, u32[]{:S(2)}) collective-permute-start(bf16[2064,128]{1,0:T(8,128)(2,1)S(1)} %get-tuple-element.20.refs_0_.refs_3_), channel_id=1, source_target_pairs={{1,17},{3,19},{5,21},{7,23},{9,25},{11,27},{13,29},{15,31},{16,0},... | collective-permute-start | bytes 1585160 | tf_op jit(solution)/shard_map/ppermute | solution.py:255
  5.2 3.5 %collective-permute-start = (bf16[2064,128]{1,0:T(8,128)(2,1)S(1)}, bf16[2064,128]{1,0:T(8,128)(2,1)S(1)}, u32[]{:S(2)}, u32[]{:S(2)}) collective-permute-start(bf16[2064,128]{1,0:T(8,128)(2,1)S(1)} %get-tuple-element.23.refs_0_.refs_3_), channel_id=1, source_target_pairs={{1,17},{3,19},{5,21},{7,23},{9,25},{11,27},{13,29},{15,31},{16,0},... | collective-permute-start | bytes 1585160 | tf_op jit(solution)/shard_map/ppermute | solution.py:255
  8.7 5.4 %collective-permute-start.3 = (bf16[2064,128]{1,0:T(8,128)(2,1)S(1)}, bf16[2064,128]{1,0:T(8,128)(2,1)S(1)}, u32[]{:S(2)}, u32[]{:S(2)}) collective-permute-start(bf16[2064,128]{1,0:T(8,128)(2,1)S(1)} %get-tuple-element.21.refs_1_), channel_id=1, source_target_pairs={{0,16},{2,18},{4,20},{6,22},{8,24},{10,26},{12,28},{14,30},{16,32}... | collective-permute-start | bytes 1585160 | tf_op jit(solution)/shard_map/ppermute | solution.py:255
  14.1 3.8 %own_a.1.refs_5_ = f32[16,128]{1,0:T(8,128)S(1)} custom-call(bf16[2064,128]{1,0:T(8,128)(2,1)S(1)} %get-tuple-element.20.refs_0_.refs_3_, bf16[2064,128]{1,0:T(8,128)(2,1)S(1)} %get-tuple-element.21.refs_1_, s32[16,128]{1,0:T(8,128)S(1)} %bitcast.4), custom_call_target="tpu_custom_call" | custom-call | flops 1073741824 | bytes 1048576 | tf_op jit(solution)/shard_map/own_a/pallas_call | solution.py:203
  17.9 0.0 collective-permute-done.1.refs_0_
  18.0 1.9 %collective-permute-start.5 = (bf16[2064,128]{1,0:T(8,128)(2,1)S(1)}, bf16[2064,128]{1,0:T(8,128)(2,1)S(1)}, u32[]{:S(2)}, u32[]{:S(2)}) collective-permute-start(bf16[2064,128]{1,0:T(8,128)(2,1)S(1)} %collective-permute-done.1.refs_0_), channel_id=1, source_target_pairs={{1,17},{3,19},{5,21},{7,23},{9,25},{11,27},{13,29},{15,31},{16,0},... | collective-permute-start | bytes 1585160 | tf_op jit(solution)/shard_map/ppermute | solution.py:255
  19.9 3.8 %own_b.1.refs_6_ = f32[16,128]{1,0:T(8,128)S(1)} custom-call(bf16[2064,128]{1,0:T(8,128)(2,1)S(1)} %get-tuple-element.23.refs_0_.refs_3_, bf16[2064,128]{1,0:T(8,128)(2,1)S(1)} %get-tuple-element.30.refs_1_, s32[16,128]{1,0:T(8,128)S(1)} %bitcast.5), custom_call_target="tpu_custom_call" | custom-call | flops 1073741824 | bytes 1048576 | tf_op jit(solution)/shard_map/own_b/pallas_call | solution.py:203
  23.7 0.0 collective-permute-done.refs_0_
  23.7 3.0 %collective-permute-start.2 = (bf16[2064,128]{1,0:T(8,128)(2,1)S(1)}, bf16[2064,128]{1,0:T(8,128)(2,1)S(1)}, u32[]{:S(2)}, u32[]{:S(2)}) collective-permute-start(bf16[2064,128]{1,0:T(8,128)(2,1)S(1)} %collective-permute-done.refs_0_), channel_id=1, source_target_pairs={{1,17},{3,19},{5,21},{7,23},{9,25},{11,27},{13,29},{15,31},{16,0},... | collective-permute-start | bytes 1585160 | tf_op jit(solution)/shard_map/ppermute | solution.py:255
  26.7 0.0 collective-permute-done.3.refs_1_.refs_2_
  26.7 7.0 %collective-permute-start.4 = (bf16[2064,128]{1,0:T(8,128)(2,1)S(1)}, bf16[2064,128]{1,0:T(8,128)(2,1)S(1)}, u32[]{:S(2)}, u32[]{:S(2)}) collective-permute-start(bf16[2064,128]{1,0:T(8,128)(2,1)S(1)} %get-tuple-element.30.refs_1_), channel_id=1, source_target_pairs={{0,16},{2,18},{4,20},{6,22},{8,24},{10,26},{12,28},{14,30},{16,32}... | collective-permute-start | bytes 1585160 | tf_op jit(solution)/shard_map/ppermute | solution.py:255
  33.7 0.0 collective-permute-done.5.refs_0_
  33.7 2.7 %middle_a.1.refs_3_.refs_8_ = f32[16,128]{1,0:T(8,128)S(1)} custom-call(bf16[2064,128]{1,0:T(8,128)(2,1)S(1)} %collective-permute-done.5.refs_0_, bf16[2064,128]{1,0:T(8,128)(2,1)S(1)} %get-tuple-element.21.refs_1_), custom_call_target="tpu_custom_call" | custom-call | flops 1073741824 | bytes 1048576 | tf_op jit(solution)/shard_map/middle_a/pallas_call | solution.py:203
  36.4 2.8 %last_a.1.refs_2_ = f32[16,128]{1,0:T(8,128)S(1)} custom-call(bf16[2064,128]{1,0:T(8,128)(2,1)S(1)} %collective-permute-done.5.refs_0_, bf16[2064,128]{1,0:T(8,128)(2,1)S(1)} %collective-permute-done.3.refs_1_.refs_2_), custom_call_target="tpu_custom_call" | custom-call | flops 1073741824 | bytes 1048576 | tf_op jit(solution)/shard_map/last_a/pallas_call | solution.py:203
  39.2 2.7 %first_a.1.refs_7_ = f32[16,128]{1,0:T(8,128)S(1)} custom-call(bf16[2064,128]{1,0:T(8,128)(2,1)S(1)} %collective-permute-done.1.refs_0_, bf16[2064,128]{1,0:T(8,128)(2,1)S(1)} %get-tuple-element.21.refs_1_, bf16[2064,128]{1,0:T(8,128)(2,1)S(1)} %collective-permute-done.3.refs_1_.refs_2_, bf16[2064,128]{1,0:T(8,128)(2,1)S(1)} %get-tuple-element.20.refs_0_.refs_3_), custom_call_target="tpu_custom_call" | custom-call | flops 1073741824 | bytes 1048576 | tf_op jit(solution)/shard_map/first_a/pallas_call | solution.py:203
  41.9 0.0 collective-permute-done.2.refs_0_.refs_4_
  41.9 2.8 %middle_b.1.refs_4_.refs_9_ = f32[16,128]{1,0:T(8,128)S(1)} custom-call(bf16[2064,128]{1,0:T(8,128)(2,1)S(1)} %collective-permute-done.2.refs_0_.refs_4_, bf16[2064,128]{1,0:T(8,128)(2,1)S(1)} %get-tuple-element.30.refs_1_), custom_call_target="tpu_custom_call" | custom-call | flops 1073741824 | bytes 1048576 | tf_op jit(solution)/shard_map/middle_b/pallas_call | solution.py:203
  44.7 0.0 collective-permute-done.4.refs_1_.refs_2_
  44.7 2.7 %last_b.1 = f32[16,128]{1,0:T(8,128)S(1)} custom-call(bf16[2064,128]{1,0:T(8,128)(2,1)S(1)} %collective-permute-done.2.refs_0_.refs_4_, bf16[2064,128]{1,0:T(8,128)(2,1)S(1)} %collective-permute-done.4.refs_1_.refs_2_, f32[16,128]{1,0:T(8,128)S(1)} %last_a.1.refs_2_, f32[16,128]{1,0:T(8,128)S(1)} %middle_a.1.refs_3_.refs_8_, ...), custom_call_target="tpu_custom_call" | custom-call | flops 1073741824 | bytes 1048576 | tf_op jit(solution)/shard_map/last_b/pallas_call | solution.py:203
  47.4 3.2 %collective-permute-start.6 = (f32[16,128]{1,0:T(8,128)S(1)}, f32[16,128]{1,0:T(8,128)S(1)}, u32[]{:S(2)}, u32[]{:S(2)}) collective-permute-start(f32[16,128]{1,0:T(8,128)S(1)} %last_b.1), channel_id=1, source_target_pairs={{16,0},{18,2},{20,4},{22,6},{24,8},{26,10},{28,12},{30,14},{32,16}... | collective-permute-start | bytes 24584 | tf_op jit(solution)/shard_map/ppermute | solution.py:255
  50.6 3.1 %near.1 = f32[16,128]{1,0:T(8,128)S(1)} custom-call(bf16[2064,128]{1,0:T(8,128)(2,1)S(1)} %collective-permute-done.refs_0_, bf16[2064,128]{1,0:T(8,128)(2,1)S(1)} %get-tuple-element.30.refs_1_, bf16[2064,128]{1,0:T(8,128)(2,1)S(1)} %collective-permute-done.4.refs_1_.refs_2_, bf16[2064,128]{1,0:T(8,128)(2,1)S(1)} %get-tuple-element.23.refs_0_.refs_3_, ...), custom_call_target="tpu_custom_call" | custom-call | flops 2147483648 | bytes 2097152 | tf_op jit(solution)/shard_map/near/pallas_call | solution.py:203
  53.7 17.3 %all_to_all.9 = f32[16,1,128]{2,1,0:T(1,128)S(1)} all-to-all(f32[16,1,128]{2,1,0:T(1,128)S(1)} %bitcast.6), channel_id=1, replica_groups=mesh['ctx'=16,'head'=16] {'head'}, dimensions={0} | all-to-all | bytes 16384 | tf_op jit(solution)/shard_map/all_to_all | solution.py:303
  71.1 0.5 reduce_sum.9
  (4 shorter events, 0.0 us)
Async XLA Ops:
  0.0 14.1 %copy-start = (s32[2048]{0:T(1024)S(1)}, s32[2048]{0:T(1024)}, u32[]{:S(2)}) copy-start(s32[2048]{0:T(1024)} %param.7) | copy-start | bytes 24580
  1.6 16.3 %collective-permute-start.1 = (bf16[2064,128]{1,0:T(8,128)(2,1)S(1)}, bf16[2064,128]{1,0:T(8,128)(2,1)S(1)}, u32[]{:S(2)}, u32[]{:S(2)}) collective-permute-start(bf16[2064,128]{1,0:T(8,128)(2,1)S(1)} %get-tuple-element.20.refs_0_.refs_3_), channel_id=1, source_target_pairs={{1,17},{3,19},{5,21},{7,23},{9,25},{11,27},{13,29},{15,31},{16,0},... | collective-permute-start | bytes 1585160 | tf_op jit(solution)/shard_map/ppermute | solution.py:255
  5.2 18.5 %collective-permute-start = (bf16[2064,128]{1,0:T(8,128)(2,1)S(1)}, bf16[2064,128]{1,0:T(8,128)(2,1)S(1)}, u32[]{:S(2)}, u32[]{:S(2)}) collective-permute-start(bf16[2064,128]{1,0:T(8,128)(2,1)S(1)} %get-tuple-element.23.refs_0_.refs_3_), channel_id=1, source_target_pairs={{1,17},{3,19},{5,21},{7,23},{9,25},{11,27},{13,29},{15,31},{16,0},... | collective-permute-start | bytes 1585160 | tf_op jit(solution)/shard_map/ppermute | solution.py:255
  8.7 17.9 %collective-permute-start.3 = (bf16[2064,128]{1,0:T(8,128)(2,1)S(1)}, bf16[2064,128]{1,0:T(8,128)(2,1)S(1)}, u32[]{:S(2)}, u32[]{:S(2)}) collective-permute-start(bf16[2064,128]{1,0:T(8,128)(2,1)S(1)} %get-tuple-element.21.refs_1_), channel_id=1, source_target_pairs={{0,16},{2,18},{4,20},{6,22},{8,24},{10,26},{12,28},{14,30},{16,32}... | collective-permute-start | bytes 1585160 | tf_op jit(solution)/shard_map/ppermute | solution.py:255
  18.0 15.7 %collective-permute-start.5 = (bf16[2064,128]{1,0:T(8,128)(2,1)S(1)}, bf16[2064,128]{1,0:T(8,128)(2,1)S(1)}, u32[]{:S(2)}, u32[]{:S(2)}) collective-permute-start(bf16[2064,128]{1,0:T(8,128)(2,1)S(1)} %collective-permute-done.1.refs_0_), channel_id=1, source_target_pairs={{1,17},{3,19},{5,21},{7,23},{9,25},{11,27},{13,29},{15,31},{16,0},... | collective-permute-start | bytes 1585160 | tf_op jit(solution)/shard_map/ppermute | solution.py:255
  23.7 18.1 %collective-permute-start.2 = (bf16[2064,128]{1,0:T(8,128)(2,1)S(1)}, bf16[2064,128]{1,0:T(8,128)(2,1)S(1)}, u32[]{:S(2)}, u32[]{:S(2)}) collective-permute-start(bf16[2064,128]{1,0:T(8,128)(2,1)S(1)} %collective-permute-done.refs_0_), channel_id=1, source_target_pairs={{1,17},{3,19},{5,21},{7,23},{9,25},{11,27},{13,29},{15,31},{16,0},... | collective-permute-start | bytes 1585160 | tf_op jit(solution)/shard_map/ppermute | solution.py:255
  26.7 18.0 %collective-permute-start.4 = (bf16[2064,128]{1,0:T(8,128)(2,1)S(1)}, bf16[2064,128]{1,0:T(8,128)(2,1)S(1)}, u32[]{:S(2)}, u32[]{:S(2)}) collective-permute-start(bf16[2064,128]{1,0:T(8,128)(2,1)S(1)} %get-tuple-element.30.refs_1_), channel_id=1, source_target_pairs={{0,16},{2,18},{4,20},{6,22},{8,24},{10,26},{12,28},{14,30},{16,32}... | collective-permute-start | bytes 1585160 | tf_op jit(solution)/shard_map/ppermute | solution.py:255
  47.4 6.3 %collective-permute-start.6 = (f32[16,128]{1,0:T(8,128)S(1)}, f32[16,128]{1,0:T(8,128)S(1)}, u32[]{:S(2)}, u32[]{:S(2)}) collective-permute-start(f32[16,128]{1,0:T(8,128)S(1)} %last_b.1), channel_id=1, source_target_pairs={{16,0},{18,2},{20,4},{22,6},{24,8},{26,10},{28,12},{30,14},{32,16}... | collective-permute-start | bytes 24584 | tf_op jit(solution)/shard_map/ppermute | solution.py:255

commit v5 on v4

--- a/solution.py
+++ b/solution.py
@@ -137,23 +137,32 @@
 
     upper = shard >= shards // 2
 
-    def copies_of(number, chosen):
+    def copies_of(number, chosen, relayed=False):
         query, key, _ = jobs[number][chosen]
+        if isinstance(query, tuple):
+            query = query[1 if relayed else 0]
         return [
             pltpu.make_async_copy(arrays[key].at[:rows], k_buf.at[number], sems.at[number, 0]),
             pltpu.make_async_copy(arrays[query].at[:rows], q_buf.at[number], sems.at[number, 1]),
             pltpu.make_async_copy(arrays[query].at[rows:], lse_buf.at[number], sems.at[number, 2]),
         ]
 
-    def start_job(number, chosen):
-        for copy in copies_of(number, chosen):
+    def start_job(number, chosen, relayed):
+        for copy in copies_of(number, chosen, relayed):
             copy.start()
 
+    at_target = shard == shards // 2 - 1
     for number, (_, _, gate) in enumerate(jobs):
         wanted = True if gate is None else gate(role, upper)
         for chosen in range(2):
-            if jobs[number][chosen] is not None:
-                pl.when((role == chosen) & wanted)(functools.partial(start_job, number, chosen))
+            entry = jobs[number][chosen]
+            if entry is None:
+                continue
+            here = (role == chosen) & wanted
+            if isinstance(entry[0], tuple):
+                pl.when(here & at_target)(functools.partial(start_job, number, chosen, True))
+                here = here & jnp.logical_not(at_target)
+            pl.when(here)(functools.partial(start_job, number, chosen, False))
     if is_own:
         first_rows = lax.broadcasted_iota(jnp.int32, (64, LANES), 0).astype(jnp.float32) * STEP
 
@@ -226,12 +235,28 @@
     return (core_0, core_1, gate)
 
 
-def runs_early(role, upper):
+def core_1(role, upper):
+    return role == 1
+
+
+def core_0(role, upper):
+    return role == 0
+
+
+def core_0_lower(role, upper):
+    return (role == 0) & jnp.logical_not(upper)
+
+
+def core_0_upper(role, upper):
+    return (role == 0) & upper
+
+
+def not_core_0_lower(role, upper):
     return (role == 1) | upper
 
 
-def runs_late(role, upper):
-    return (role == 0) & jnp.logical_not(upper)
+def not_core_0_upper(role, upper):
+    return (role == 1) | jnp.logical_not(upper)
 
 
 def finish_far(role, mass, small):
@@ -255,6 +280,25 @@
     return lax.ppermute(value, ("ctx", "head"), pairs)
 
 
+def move_around(value, mesh_shape):
+    shards, heads = mesh_shape
+    pairs = []
+    for shard in range(shards):
+        for head in range(heads):
+            if head % 2 == 1 and shard == shards // 2:
+                pairs.append((shard * heads + head, head - 1))
+            elif head % 2 == 1 and shard > 0:
+                pairs.append((shard * heads + head, (shard - 1) * heads + head))
+    return lax.ppermute(value, ("ctx", "head"), pairs)
+
+
+def move_on(value, mesh_shape):
+    shards, heads = mesh_shape
+    target = shards // 2 - 1
+    pairs = [(head, target * heads + head + 1) for head in range(0, heads, 2)]
+    return lax.ppermute(value, ("ctx", "head"), pairs)
+
+
 def after(value, *done):
     return lax.optimization_barrier((value, *done))[0]
 
@@ -266,25 +310,40 @@
     offsets = query_offsets.reshape(rows // LANES, LANES)
     own = [job((0, 1, 0), (1, 0, 0))]
     middle = [job((0, 1, 2), (1, 0, 0))]
+    last_relayed = [job((0, 1, 2), ((2, 3), 0, 1))]
     last = [job((0, 1, 2), (1, 0, 1))]
-    middle_early = [job((0, 1, 2), (1, 0, 0), runs_early)]
-    first = [job((0, 1, 1), (2, 3, 1))]
-    near_jobs = [job((0, 1, 1), (2, 3, 1)), job((4, 1, 2), None, runs_late)]
+    first_early = [job((0, 1, 1), ((2, 4), 3, 1), not_core_0_lower)]
+    middle_early = [job(None, (1, 0, 0), core_1), job((2, 1, 1), None, core_0_upper)]
+    near_jobs = [
+        job((0, 1, 1), (2, 3, 1), not_core_0_upper),
+        job((4, 1, 2), None, core_0),
+        job((5, 6, 1), None, core_0_lower),
+    ]
 
     xa1 = move(xa0, mesh_shape, out)
     xb1 = move(xb0, mesh_shape, out)
-    za1 = move(za0, mesh_shape, back)
+    za1_core_1 = move_around(za0, mesh_shape)
+    za1_core_0 = move(za0, mesh_shape, (1, 0))
     own_a = mass_call("own_a", [xa0, za0], own, (offsets,), is_own=True)
     xa1 = after(xa1, own_a)
     xa2 = move(xa1, mesh_shape, out)
-    own_b = mass_call("own_b", [after(xb0, xa1), zb0], own, (offsets,), is_own=True)
-    xb1 = after(xb1, own_b)
+    xb1 = after(xb1, xa1)
     xb2 = move(xb1, mesh_shape, out)
-    zb1 = move(after(zb0, xb1, za1), mesh_shape, back)
-    middle_a = mass_call("middle_a", [after(xa2, xb1, za1), za0], middle)
-    last_a = mass_call("last_a", [after(xa2, middle_a), za1], last)
-    first_a = mass_call("first_a", [after(xa1, last_a), za0, za1, xa0], first)
-    middle_b = mass_call("middle_b", [xb2, after(zb0, first_a)], middle_early)
+    za1_core_1 = after(za1_core_1, xb1)
+    za1_relayed = move_on(za1_core_1, mesh_shape)
+    zb0 = after(zb0, xb1, za1_core_1)
+    zb1 = move(zb0, mesh_shape, back)
+    own_b = mass_call("own_b", [after(xb0, za1_core_0), zb0], own, (offsets,), is_own=True)
+    middle_a = mass_call("middle_a", [after(xa2, own_b), za0], middle)
+    last_a = mass_call(
+        "last_a",
+        [after(xa2, middle_a), za1_core_0, za1_core_1, za1_relayed],
+        last_relayed,
+    )
+    first_a = mass_call(
+        "first_a", [after(xa1, last_a), za0, za1_core_1, xa0, za1_relayed], first_early
+    )
+    middle_b = mass_call("middle_b", [xb2, after(zb0, first_a), xb1], middle_early)
     far = mass_call(
         "last_b",
         [xb2, after(zb1, middle_b)],
@@ -294,7 +353,7 @@
     )
     local = mass_call(
         "near",
-        [after(xb1, far), zb0, zb1, xb0, xb2],
+        [after(xb1, far), zb0, zb1, xb0, xb2, xa1, za0],
         near_jobs,
         (own_a, own_b, first_a, middle_a, middle_b),
         finish=finish_near,

time: 71.9 us -> 71.3 us (level)
  waiting for transfers between devices: 0.02 us -> 4.92 us
  blocking collectives: 17.3 us -> 13.6 us
  starting transfers between devices: 27.5 us -> 25.4 us
    ppermute x7, starting transfers between devices: 27.5 us -> 22.8 us  [move(): return lax.ppermute(value, ('ctx', 'head'), pairs)]
    all_to_all x1, blocking collectives: 17.3 us -> 13.6 us  [on_device(): spread = lax.all_to_all(local, 'head', 0, 0, tiled=True)]
    ppermute x7, waiting for transfers between devices: 0.02 us -> 2.67 us  [move(): return lax.ppermute(value, ('ctx', 'head'), pairs)]
    ppermute x0 -> x2, starting transfers between devices: none -> 2.6 us  [the longest x1 1.92 us: move_around(): return lax.ppermute(value, ('ctx', 'head'), pairs)]
    ppermute x0 -> x2, waiting for transfers between devices: none -> 2.24 us  [the longest x1 2.24 us: move_around(): return lax.ppermute(value, ('ctx', 'head'), pairs)]
  transfers between devices with their start and end apart: 7 -> 9, of which waited for: 0 -> 3; matrix products, arithmetic and copies ran while one was open for 0% -> 0% of each run, Pallas kernels for 30% -> 31%
where the time goes in v5:
time: 71.3 us; the launch traced here: 71 us
  Pallas kernels  26.3 us (37%)
  starting transfers between devices  25.4 us (36%)
  blocking collectives  13.6 us (19%)
  waiting for transfers between devices  4.92 us (7%)
    pallas_call x8, Pallas kernels, mass_call(): pl.pallas_call(functools.partial(mass_kernel, jobs, len(arrays), len(smal...  24.6 us
    ppermute x7, starting transfers between devices, move(): return lax.ppermute(value, ('ctx', 'head'), pairs)  22.8 us
    all_to_all x1, blocking collectives, on_device(): spread = lax.all_to_all(local, 'head', 0, 0, tiled=True)  13.6 us
    ppermute x7, waiting for transfers between devices, move(): return lax.ppermute(value, ('ctx', 'head'), pairs)  2.67 us
    ppermute x1, waiting for transfers between devices, move_around(): return lax.ppermute(value, ('ctx', 'head'), pairs)  2.24 us
    ppermute x1, starting transfers between devices, move_around(): return lax.ppermute(value, ('ctx', 'head'), pairs)  1.92 us
    pallas_call x1, Pallas kernels, prepare(): pl.pallas_call(prepare_kernel, out_shape=(half,) * 4, in_specs=[pl.BlockS...  1.63 us
  transfers between devices with their start and end apart: 9, of which 3 were waited for; matrix products, arithmetic and copies ran while one was open for 0% of the time, Pallas kernels for 31%

profile of v5, /device:TPU:17, one launch (start us, length us, event | category | flops | bytes accessed | tf_op | source)
XLA Modules:
  0.0 71.0 jit_solution(3909520553046319730)
XLA Ops:
  0.0 1.6 %prepare.1 = (bf16[2064,128]{1,0:T(8,128)(2,1)S(1)}, bf16[2064,128]{1,0:T(8,128)(2,1)S(1)}, bf16[2064,128]{1,0:T(8,128)(2,1)S(1)}, bf16[2064,128]{1,0:T(8,128)(2,1)S(1)}) custom-call(bf16[2048,256]{1,0:T(8,128)(2,1)} %q_ref.1, bf16[2048,256]{1,0:T(8,128)(2,1)} %k_ref.1, bf16[2,2048]{1,0:T(2,128)(2,1)} %lse_ref.1), custom_call_target="tpu_custom_call" | custom-call | tf_op jit(solution)/shard_map/prepare/pallas_call | solution.py:68
  1.6 3.5 %collective-permute-start.1 = (bf16[2064,128]{1,0:T(8,128)(2,1)S(1)}, bf16[2064,128]{1,0:T(8,128)(2,1)S(1)}, u32[]{:S(2)}, u32[]{:S(2)}) collective-permute-start(bf16[2064,128]{1,0:T(8,128)(2,1)S(1)} %get-tuple-element.21.refs_0_.refs_3_), channel_id=1, source_target_pairs={{1,17},{3,19},{5,21},{7,23},{9,25},{11,27},{13,29},{15,31},{16,0},... | collective-permute-start | bytes 1585160 | tf_op jit(solution)/shard_map/ppermute | solution.py:280
  5.2 3.5 %collective-permute-start = (bf16[2064,128]{1,0:T(8,128)(2,1)S(1)}, bf16[2064,128]{1,0:T(8,128)(2,1)S(1)}, u32[]{:S(2)}, u32[]{:S(2)}) collective-permute-start(bf16[2064,128]{1,0:T(8,128)(2,1)S(1)} %get-tuple-element.28.refs_0_.refs_3_), channel_id=1, source_target_pairs={{1,17},{3,19},{5,21},{7,23},{9,25},{11,27},{13,29},{15,31},{16,0},... | collective-permute-start | bytes 1585160 | tf_op jit(solution)/shard_map/ppermute | solution.py:280
  8.7 1.9 %collective-permute-start.3 = (bf16[2064,128]{1,0:T(8,128)(2,1)S(1)}, bf16[2064,128]{1,0:T(8,128)(2,1)S(1)}, u32[]{:S(2)}, u32[]{:S(2)}) collective-permute-start(bf16[2064,128]{1,0:T(8,128)(2,1)S(1)} %get-tuple-element.22.refs_1_.refs_6_), channel_id=1, source_target_pairs={{17,1},{19,3},{21,5},{23,7},{25,9},{27,11},{29,13},{31,15},{33,17}... | collective-permute-start | bytes 1585160 | tf_op jit(solution)/shard_map/ppermute | solution.py:292
  10.7 0.7 collective-permute-start.6
  11.4 3.8 %own_a.1.refs_7_ = f32[16,128]{1,0:T(8,128)S(1)} custom-call(bf16[2064,128]{1,0:T(8,128)(2,1)S(1)} %get-tuple-element.21.refs_0_.refs_3_, bf16[2064,128]{1,0:T(8,128)(2,1)S(1)} %get-tuple-element.22.refs_1_.refs_6_, s32[16,128]{1,0:T(8,128)S(1)} %bitcast.4), custom_call_target="tpu_custom_call" | custom-call | flops 1073741824 | bytes 1048576 | tf_op jit(solution)/shard_map/own_a/pallas_call | solution.py:212
  15.2 0.3 collective-permute-done.1.refs_0_.refs_5_
  15.5 3.3 %collective-permute-start.5 = (bf16[2064,128]{1,0:T(8,128)(2,1)S(1)}, bf16[2064,128]{1,0:T(8,128)(2,1)S(1)}, u32[]{:S(2)}, u32[]{:S(2)}) collective-permute-start(bf16[2064,128]{1,0:T(8,128)(2,1)S(1)} %collective-permute-done.1.refs_0_.refs_5_), channel_id=1, source_target_pairs={{1,17},{3,19},{5,21},{7,23},{9,25},{11,27},{13,29},{15,31},{16,0},... | collective-permute-start | bytes 1585160 | tf_op jit(solution)/shard_map/ppermute | solution.py:280
  18.8 2.4 %collective-permute-done.refs_2_.refs_0_ = bf16[2064,128]{1,0:T(8,128)(2,1)S(1)} collective-permute-done((bf16[2064,128]{1,0:T(8,128)(2,1)S(1)}, bf16[2064,128]{1,0:T(8,128)(2,1)S(1)}, u32[]{:S(2)}, u32[]{:S(2)}) %collective-permute-start) | collective-permute-done | bytes 528416 | tf_op jit(solution)/shard_map/ppermute | solution.py:280
  21.2 2.2 %collective-permute-done.3.refs_2_ = bf16[2064,128]{1,0:T(8,128)(2,1)S(1)} collective-permute-done((bf16[2064,128]{1,0:T(8,128)(2,1)S(1)}, bf16[2064,128]{1,0:T(8,128)(2,1)S(1)}, u32[]{:S(2)}, u32[]{:S(2)}) %collective-permute-start.3) | collective-permute-done | bytes 528416 | tf_op jit(solution)/shard_map/ppermute | solution.py:292
  23.4 0.7 collective-permute-start.7
  24.1 5.4 %collective-permute-start.2 = (bf16[2064,128]{1,0:T(8,128)(2,1)S(1)}, bf16[2064,128]{1,0:T(8,128)(2,1)S(1)}, u32[]{:S(2)}, u32[]{:S(2)}) collective-permute-start(bf16[2064,128]{1,0:T(8,128)(2,1)S(1)} %collective-permute-done.refs_2_.refs_0_), channel_id=1, source_target_pairs={{1,17},{3,19},{5,21},{7,23},{9,25},{11,27},{13,29},{15,31},{16,0},... | collective-permute-start | bytes 1585160 | tf_op jit(solution)/shard_map/ppermute | solution.py:280
  29.5 0.0 collective-permute-done.6.refs_1_
  29.5 3.5 %collective-permute-start.4 = (bf16[2064,128]{1,0:T(8,128)(2,1)S(1)}, bf16[2064,128]{1,0:T(8,128)(2,1)S(1)}, u32[]{:S(2)}, u32[]{:S(2)}) collective-permute-start(bf16[2064,128]{1,0:T(8,128)(2,1)S(1)} %get-tuple-element.32.refs_1_), channel_id=1, source_target_pairs={{0,16},{2,18},{4,20},{6,22},{8,24},{10,26},{12,28},{14,30},{16,32}... | collective-permute-start | bytes 1585160 | tf_op jit(solution)/shard_map/ppermute | solution.py:280
  33.0 3.8 %own_b.1.refs_8_ = f32[16,128]{1,0:T(8,128)S(1)} custom-call(bf16[2064,128]{1,0:T(8,128)(2,1)S(1)} %get-tuple-element.28.refs_0_.refs_3_, bf16[2064,128]{1,0:T(8,128)(2,1)S(1)} %get-tuple-element.32.refs_1_, s32[16,128]{1,0:T(8,128)S(1)} %bitcast.5), custom_call_target="tpu_custom_call" | custom-call | flops 1073741824 | bytes 1048576 | tf_op jit(solution)/shard_map/own_b/pallas_call | solution.py:212
  36.9 2.7 %middle_a.1.refs_3_.refs_10_ = f32[16,128]{1,0:T(8,128)S(1)} custom-call(bf16[2064,128]{1,0:T(8,128)(2,1)S(1)} %collective-permute-done.5.refs_0_, bf16[2064,128]{1,0:T(8,128)(2,1)S(1)} %get-tuple-element.22.refs_1_.refs_6_), custom_call_target="tpu_custom_call" | custom-call | flops 1073741824 | bytes 1048576 | tf_op jit(solution)/shard_map/middle_a/pallas_call | solution.py:212
  39.5 2.8 %last_a.1.refs_2_ = f32[16,128]{1,0:T(8,128)S(1)} custom-call(bf16[2064,128]{1,0:T(8,128)(2,1)S(1)} %collective-permute-done.5.refs_0_, bf16[2064,128]{1,0:T(8,128)(2,1)S(1)} %collective-permute-done.6.refs_1_, bf16[2064,128]{1,0:T(8,128)(2,1)S(1)} %collective-permute-done.3.refs_2_, bf16[2064,128]{1,0:T(8,128)(2,1)S(1)} %collective-permute-done.7.refs_3_.refs_4_), custom_call_target="tpu_custom_call" | custom-call | flops 1073741824 | bytes 1048576 | tf_op jit(solution)/shard_map/last_a/pallas_call | solution.py:212
  42.4 2.8 %first_a.1.refs_9_ = f32[16,128]{1,0:T(8,128)S(1)} custom-call(bf16[2064,128]{1,0:T(8,128)(2,1)S(1)} %collective-permute-done.1.refs_0_.refs_5_, bf16[2064,128]{1,0:T(8,128)(2,1)S(1)} %get-tuple-element.22.refs_1_.refs_6_, bf16[2064,128]{1,0:T(8,128)(2,1)S(1)} %collective-permute-done.3.refs_2_, bf16[2064,128]{1,0:T(8,128)(2,1)S(1)} %get-tuple-element.21.refs_0_.refs_3_, ...), custom_call_target="tpu_custom_call" | custom-call | flops 1073741824 | bytes 1048576 | tf_op jit(solution)/shard_map/first_a/pallas_call | solution.py:212
  45.2 2.9 %middle_b.1.refs_4_.refs_11_ = f32[16,128]{1,0:T(8,128)S(1)} custom-call(bf16[2064,128]{1,0:T(8,128)(2,1)S(1)} %collective-permute-done.2.refs_0_.refs_4_, bf16[2064,128]{1,0:T(8,128)(2,1)S(1)} %get-tuple-element.32.refs_1_, bf16[2064,128]{1,0:T(8,128)(2,1)S(1)} %collective-permute-done.refs_2_.refs_0_), custom_call_target="tpu_custom_call" | custom-call | flops 2147483648 | bytes 2097152 | tf_op jit(solution)/shard_map/middle_b/pallas_call | solution.py:212
  48.1 2.9 %last_b.1 = f32[16,128]{1,0:T(8,128)S(1)} custom-call(bf16[2064,128]{1,0:T(8,128)(2,1)S(1)} %collective-permute-done.2.refs_0_.refs_4_, bf16[2064,128]{1,0:T(8,128)(2,1)S(1)} %collective-permute-done.4.refs_1_.refs_2_, f32[16,128]{1,0:T(8,128)S(1)} %last_a.1.refs_2_, f32[16,128]{1,0:T(8,128)S(1)} %middle_a.1.refs_3_.refs_10_, ...), custom_call_target="tpu_custom_call" | custom-call | flops 1073741824 | bytes 1048576 | tf_op jit(solution)/shard_map/last_b/pallas_call | solution.py:212
  51.0 2.9 %collective-permute-start.8 = (f32[16,128]{1,0:T(8,128)S(1)}, f32[16,128]{1,0:T(8,128)S(1)}, u32[]{:S(2)}, u32[]{:S(2)}) collective-permute-start(f32[16,128]{1,0:T(8,128)S(1)} %last_b.1), channel_id=1, source_target_pairs={{16,0},{18,2},{20,4},{22,6},{24,8},{26,10},{28,12},{30,14},{32,16}... | collective-permute-start | bytes 24584 | tf_op jit(solution)/shard_map/ppermute | solution.py:280
  53.9 2.9 %near.1 = f32[16,128]{1,0:T(8,128)S(1)} custom-call(bf16[2064,128]{1,0:T(8,128)(2,1)S(1)} %collective-permute-done.refs_2_.refs_0_, bf16[2064,128]{1,0:T(8,128)(2,1)S(1)} %get-tuple-element.32.refs_1_, bf16[2064,128]{1,0:T(8,128)(2,1)S(1)} %collective-permute-done.4.refs_1_.refs_2_, bf16[2064,128]{1,0:T(8,128)(2,1)S(1)} %get-tuple-element.28.refs_0_.refs_3_, ...), custom_call_target="tpu_custom_call" | custom-call | flops 3221225472 | bytes 3145728 | tf_op jit(solution)/shard_map/near/pallas_call | solution.py:212
  56.8 13.6 %all_to_all.9 = f32[16,1,128]{2,1,0:T(1,128)S(1)} all-to-all(f32[16,1,128]{2,1,0:T(1,128)S(1)} %bitcast.6), channel_id=1, replica_groups=mesh['ctx'=16,'head'=16] {'head'}, dimensions={0} | all-to-all | bytes 16384 | tf_op jit(solution)/shard_map/all_to_all | solution.py:362
  70.5 0.5 reduce_sum.9
  (8 shorter events, 0.0 us)
Async XLA Ops:
  0.0 11.4 %copy-start = (s32[2048]{0:T(1024)S(1)}, s32[2048]{0:T(1024)}, u32[]{:S(2)}) copy-start(s32[2048]{0:T(1024)} %param.7) | copy-start | bytes 24580
  1.6 13.9 %collective-permute-start.1 = (bf16[2064,128]{1,0:T(8,128)(2,1)S(1)}, bf16[2064,128]{1,0:T(8,128)(2,1)S(1)}, u32[]{:S(2)}, u32[]{:S(2)}) collective-permute-start(bf16[2064,128]{1,0:T(8,128)(2,1)S(1)} %get-tuple-element.21.refs_0_.refs_3_), channel_id=1, source_target_pairs={{1,17},{3,19},{5,21},{7,23},{9,25},{11,27},{13,29},{15,31},{16,0},... | collective-permute-start | bytes 1585160 | tf_op jit(solution)/shard_map/ppermute | solution.py:280
  5.2 16.0 %collective-permute-start = (bf16[2064,128]{1,0:T(8,128)(2,1)S(1)}, bf16[2064,128]{1,0:T(8,128)(2,1)S(1)}, u32[]{:S(2)}, u32[]{:S(2)}) collective-permute-start(bf16[2064,128]{1,0:T(8,128)(2,1)S(1)} %get-tuple-element.28.refs_0_.refs_3_), channel_id=1, source_target_pairs={{1,17},{3,19},{5,21},{7,23},{9,25},{11,27},{13,29},{15,31},{16,0},... | collective-permute-start | bytes 1585160 | tf_op jit(solution)/shard_map/ppermute | solution.py:280
  8.7 14.7 %collective-permute-start.3 = (bf16[2064,128]{1,0:T(8,128)(2,1)S(1)}, bf16[2064,128]{1,0:T(8,128)(2,1)S(1)}, u32[]{:S(2)}, u32[]{:S(2)}) collective-permute-start(bf16[2064,128]{1,0:T(8,128)(2,1)S(1)} %get-tuple-element.22.refs_1_.refs_6_), channel_id=1, source_target_pairs={{17,1},{19,3},{21,5},{23,7},{25,9},{27,11},{29,13},{31,15},{33,17}... | collective-permute-start | bytes 1585160 | tf_op jit(solution)/shard_map/ppermute | solution.py:292
  10.7 18.8 %collective-permute-start.6 = (bf16[2064,128]{1,0:T(8,128)(2,1)S(1)}, bf16[2064,128]{1,0:T(8,128)(2,1)S(1)}, u32[]{:S(2)}, u32[]{:S(2)}) collective-permute-start(bf16[2064,128]{1,0:T(8,128)(2,1)S(1)} %get-tuple-element.22.refs_1_.refs_6_), channel_id=1, source_target_pairs={{0,16},{2,18},{4,20},{6,22},{8,24},{10,26},{12,28},{14,30},{16,32}... | collective-permute-start | bytes 1585160 | tf_op jit(solution)/shard_map/ppermute | solution.py:280
  15.5 21.4 %collective-permute-start.5 = (bf16[2064,128]{1,0:T(8,128)(2,1)S(1)}, bf16[2064,128]{1,0:T(8,128)(2,1)S(1)}, u32[]{:S(2)}, u32[]{:S(2)}) collective-permute-start(bf16[2064,128]{1,0:T(8,128)(2,1)S(1)} %collective-permute-done.1.refs_0_.refs_5_), channel_id=1, source_target_pairs={{1,17},{3,19},{5,21},{7,23},{9,25},{11,27},{13,29},{15,31},{16,0},... | collective-permute-start | bytes 1585160 | tf_op jit(solution)/shard_map/ppermute | solution.py:280
  23.4 16.1 %collective-permute-start.7 = (bf16[2064,128]{1,0:T(8,128)(2,1)S(1)}, bf16[2064,128]{1,0:T(8,128)(2,1)S(1)}, u32[]{:S(2)}, u32[]{:S(2)}) collective-permute-start(bf16[2064,128]{1,0:T(8,128)(2,1)S(1)} %collective-permute-done.3.refs_2_), channel_id=1, source_target_pairs={{0,113},{2,115},{4,117},{6,119},{8,121},{10,123},{12,125},{14,127}} | collective-permute-start | bytes 1585160 | tf_op jit(solution)/shard_map/ppermute | solution.py:299
  24.1 21.1 %collective-permute-start.2 = (bf16[2064,128]{1,0:T(8,128)(2,1)S(1)}, bf16[2064,128]{1,0:T(8,128)(2,1)S(1)}, u32[]{:S(2)}, u32[]{:S(2)}) collective-permute-start(bf16[2064,128]{1,0:T(8,128)(2,1)S(1)} %collective-permute-done.refs_2_.refs_0_), channel_id=1, source_target_pairs={{1,17},{3,19},{5,21},{7,23},{9,25},{11,27},{13,29},{15,31},{16,0},... | collective-permute-start | bytes 1585160 | tf_op jit(solution)/shard_map/ppermute | solution.py:280
  29.5 18.6 %collective-permute-start.4 = (bf16[2064,128]{1,0:T(8,128)(2,1)S(1)}, bf16[2064,128]{1,0:T(8,128)(2,1)S(1)}, u32[]{:S(2)}, u32[]{:S(2)}) collective-permute-start(bf16[2064,128]{1,0:T(8,128)(2,1)S(1)} %get-tuple-element.32.refs_1_), channel_id=1, source_target_pairs={{0,16},{2,18},{4,20},{6,22},{8,24},{10,26},{12,28},{14,30},{16,32}... | collective-permute-start | bytes 1585160 | tf_op jit(solution)/shard_map/ppermute | solution.py:280
  51.0 5.8 %collective-permute-start.8 = (f32[16,128]{1,0:T(8,128)S(1)}, f32[16,128]{1,0:T(8,128)S(1)}, u32[]{:S(2)}, u32[]{:S(2)}) collective-permute-start(f32[16,128]{1,0:T(8,128)S(1)} %last_b.1), channel_id=1, source_target_pairs={{16,0},{18,2},{20,4},{22,6},{24,8},{26,10},{28,12},{30,14},{32,16}... | collective-permute-start | bytes 24584 | tf_op jit(solution)/shard_map/ppermute | solution.py:280

commit v6 on v5

--- a/solution.py
+++ b/solution.py
@@ -235,24 +235,16 @@
     return (core_0, core_1, gate)
 
 
+def core_0(role, upper):
+    return role == 0
+
+
 def core_1(role, upper):
     return role == 1
 
 
-def core_0(role, upper):
-    return role == 0
-
-
-def core_0_lower(role, upper):
-    return (role == 0) & jnp.logical_not(upper)
-
-
 def core_0_upper(role, upper):
     return (role == 0) & upper
-
-
-def not_core_0_lower(role, upper):
-    return (role == 1) | upper
 
 
 def not_core_0_upper(role, upper):
@@ -312,12 +304,15 @@
     middle = [job((0, 1, 2), (1, 0, 0))]
     last_relayed = [job((0, 1, 2), ((2, 3), 0, 1))]
     last = [job((0, 1, 2), (1, 0, 1))]
-    first_early = [job((0, 1, 1), ((2, 4), 3, 1), not_core_0_lower)]
-    middle_early = [job(None, (1, 0, 0), core_1), job((2, 1, 1), None, core_0_upper)]
+    first_early = [job((0, 1, 1), None, core_0)]
+    middle_early = [
+        job(None, (1, 0, 0), core_1),
+        job((2, 1, 1), None, core_0_upper),
+    ]
     near_jobs = [
         job((0, 1, 1), (2, 3, 1), not_core_0_upper),
         job((4, 1, 2), None, core_0),
-        job((5, 6, 1), None, core_0_lower),
+        job(None, ((5, 6), 7, 1), core_1),
     ]
 
     xa1 = move(xa0, mesh_shape, out)
@@ -327,7 +322,8 @@
     own_a = mass_call("own_a", [xa0, za0], own, (offsets,), is_own=True)
     xa1 = after(xa1, own_a)
     xa2 = move(xa1, mesh_shape, out)
-    xb1 = after(xb1, xa1)
+    first_a = mass_call("first_a", [xa1, za0], first_early)
+    xb1 = after(xb1, first_a)
     xb2 = move(xb1, mesh_shape, out)
     za1_core_1 = after(za1_core_1, xb1)
     za1_relayed = move_on(za1_core_1, mesh_shape)
@@ -340,10 +336,7 @@
         [after(xa2, middle_a), za1_core_0, za1_core_1, za1_relayed],
         last_relayed,
     )
-    first_a = mass_call(
-        "first_a", [after(xa1, last_a), za0, za1_core_1, xa0, za1_relayed], first_early
-    )
-    middle_b = mass_call("middle_b", [xb2, after(zb0, first_a), xb1], middle_early)
+    middle_b = mass_call("middle_b", [xb2, after(zb0, last_a), xb1], middle_early)
     far = mass_call(
         "last_b",
         [xb2, after(zb1, middle_b)],
@@ -353,7 +346,7 @@
     )
     local = mass_call(
         "near",
-        [after(xb1, far), zb0, zb1, xb0, xb2, xa1, za0],
+        [after(xb1, far), zb0, zb1, xb0, xb2, za1_core_1, za1_relayed, xa0],
         near_jobs,
         (own_a, own_b, first_a, middle_a, middle_b),
         finish=finish_near,

time: 71.3 us -> 71.3 us (level)
  transfers between devices with their start and end apart: 9 -> 9, of which waited for: 3 -> 4; matrix products, arithmetic and copies ran while one was open for 0% -> 0% of each run, Pallas kernels for 31% -> 31%
where the time goes in v6:
time: 71.3 us; the launch traced here: 71 us
  Pallas kernels  26.3 us (37%)
  starting transfers between devices  25.2 us (35%)
  blocking collectives  13.6 us (19%)
  waiting for transfers between devices  5.09 us (7%)
    pallas_call x8, Pallas kernels, mass_call(): pl.pallas_call(functools.partial(mass_kernel, jobs, len(arrays), len(smal...  24.7 us
    ppermute x7, starting transfers between devices, move(): return lax.ppermute(value, ('ctx', 'head'), pairs)  22.6 us
    all_to_all x1, blocking collectives, on_device(): spread = lax.all_to_all(local, 'head', 0, 0, tiled=True)  13.6 us
    ppermute x7, waiting for transfers between devices, move(): return lax.ppermute(value, ('ctx', 'head'), pairs)  2.85 us
    ppermute x1, waiting for transfers between devices, move_around(): return lax.ppermute(value, ('ctx', 'head'), pairs)  2.24 us
    ppermute x1, starting transfers between devices, move_around(): return lax.ppermute(value, ('ctx', 'head'), pairs)  1.92 us
    pallas_call x1, Pallas kernels, prepare(): pl.pallas_call(prepare_kernel, out_shape=(half,) * 4, in_specs=[pl.BlockS...  1.63 us
  transfers between devices with their start and end apart: 9, of which 4 were waited for; matrix products, arithmetic and copies ran while one was open for 0% of the time, Pallas kernels for 31%

profile of v6, /device:TPU:17, one launch (start us, length us, event | category | flops | bytes accessed | tf_op | source)
XLA Modules:
  0.0 71.0 jit_solution(18109242467673343011)
XLA Ops:
  0.0 1.6 %prepare.1 = (bf16[2064,128]{1,0:T(8,128)(2,1)S(1)}, bf16[2064,128]{1,0:T(8,128)(2,1)S(1)}, bf16[2064,128]{1,0:T(8,128)(2,1)S(1)}, bf16[2064,128]{1,0:T(8,128)(2,1)S(1)}) custom-call(bf16[2048,256]{1,0:T(8,128)(2,1)} %q_ref.1, bf16[2048,256]{1,0:T(8,128)(2,1)} %k_ref.1, bf16[2,2048]{1,0:T(2,128)(2,1)} %lse_ref.1), custom_call_target="tpu_custom_call" | custom-call | tf_op jit(solution)/shard_map/prepare/pallas_call | solution.py:68
  1.6 3.5 %collective-permute-start.1 = (bf16[2064,128]{1,0:T(8,128)(2,1)S(1)}, bf16[2064,128]{1,0:T(8,128)(2,1)S(1)}, u32[]{:S(2)}, u32[]{:S(2)}) collective-permute-start(bf16[2064,128]{1,0:T(8,128)(2,1)S(1)} %get-tuple-element.20.refs_0_.refs_7_), channel_id=1, source_target_pairs={{1,17},{3,19},{5,21},{7,23},{9,25},{11,27},{13,29},{15,31},{16,0},... | collective-permute-start | bytes 1585160 | tf_op jit(solution)/shard_map/ppermute | solution.py:272
  5.2 3.5 %collective-permute-start = (bf16[2064,128]{1,0:T(8,128)(2,1)S(1)}, bf16[2064,128]{1,0:T(8,128)(2,1)S(1)}, u32[]{:S(2)}, u32[]{:S(2)}) collective-permute-start(bf16[2064,128]{1,0:T(8,128)(2,1)S(1)} %get-tuple-element.27.refs_0_.refs_3_), channel_id=1, source_target_pairs={{1,17},{3,19},{5,21},{7,23},{9,25},{11,27},{13,29},{15,31},{16,0},... | collective-permute-start | bytes 1585160 | tf_op jit(solution)/shard_map/ppermute | solution.py:272
  8.7 1.9 %collective-permute-start.3 = (bf16[2064,128]{1,0:T(8,128)(2,1)S(1)}, bf16[2064,128]{1,0:T(8,128)(2,1)S(1)}, u32[]{:S(2)}, u32[]{:S(2)}) collective-permute-start(bf16[2064,128]{1,0:T(8,128)(2,1)S(1)} %get-tuple-element.21.refs_1_), channel_id=1, source_target_pairs={{17,1},{19,3},{21,5},{23,7},{25,9},{27,11},{29,13},{31,15},{33,17}... | collective-permute-start | bytes 1585160 | tf_op jit(solution)/shard_map/ppermute | solution.py:284
  10.7 0.7 collective-permute-start.6
  11.4 3.8 %own_a.1.refs_8_ = f32[16,128]{1,0:T(8,128)S(1)} custom-call(bf16[2064,128]{1,0:T(8,128)(2,1)S(1)} %get-tuple-element.20.refs_0_.refs_7_, bf16[2064,128]{1,0:T(8,128)(2,1)S(1)} %get-tuple-element.21.refs_1_, s32[16,128]{1,0:T(8,128)S(1)} %bitcast.4), custom_call_target="tpu_custom_call" | custom-call | flops 1073741824 | bytes 1048576 | tf_op jit(solution)/shard_map/own_a/pallas_call | solution.py:212
  15.2 0.3 collective-permute-done.1.refs_0_
  15.5 3.3 %collective-permute-start.5 = (bf16[2064,128]{1,0:T(8,128)(2,1)S(1)}, bf16[2064,128]{1,0:T(8,128)(2,1)S(1)}, u32[]{:S(2)}, u32[]{:S(2)}) collective-permute-start(bf16[2064,128]{1,0:T(8,128)(2,1)S(1)} %collective-permute-done.1.refs_0_), channel_id=1, source_target_pairs={{1,17},{3,19},{5,21},{7,23},{9,25},{11,27},{13,29},{15,31},{16,0},... | collective-permute-start | bytes 1585160 | tf_op jit(solution)/shard_map/ppermute | solution.py:272
  18.8 0.5 first_a.1.refs_10_
  19.3 1.9 %collective-permute-done.refs_2_.refs_0_ = bf16[2064,128]{1,0:T(8,128)(2,1)S(1)} collective-permute-done((bf16[2064,128]{1,0:T(8,128)(2,1)S(1)}, bf16[2064,128]{1,0:T(8,128)(2,1)S(1)}, u32[]{:S(2)}, u32[]{:S(2)}) %collective-permute-start) | collective-permute-done | bytes 528416 | tf_op jit(solution)/shard_map/ppermute | solution.py:272
  21.2 2.2 %collective-permute-done.3.refs_2_.refs_5_ = bf16[2064,128]{1,0:T(8,128)(2,1)S(1)} collective-permute-done((bf16[2064,128]{1,0:T(8,128)(2,1)S(1)}, bf16[2064,128]{1,0:T(8,128)(2,1)S(1)}, u32[]{:S(2)}, u32[]{:S(2)}) %collective-permute-start.3) | collective-permute-done | bytes 528416 | tf_op jit(solution)/shard_map/ppermute | solution.py:284
  23.4 0.7 collective-permute-start.7
  24.1 5.4 %collective-permute-start.2 = (bf16[2064,128]{1,0:T(8,128)(2,1)S(1)}, bf16[2064,128]{1,0:T(8,128)(2,1)S(1)}, u32[]{:S(2)}, u32[]{:S(2)}) collective-permute-start(bf16[2064,128]{1,0:T(8,128)(2,1)S(1)} %collective-permute-done.refs_2_.refs_0_), channel_id=1, source_target_pairs={{1,17},{3,19},{5,21},{7,23},{9,25},{11,27},{13,29},{15,31},{16,0},... | collective-permute-start | bytes 1585160 | tf_op jit(solution)/shard_map/ppermute | solution.py:272
  29.5 3.5 %collective-permute-start.4 = (bf16[2064,128]{1,0:T(8,128)(2,1)S(1)}, bf16[2064,128]{1,0:T(8,128)(2,1)S(1)}, u32[]{:S(2)}, u32[]{:S(2)}) collective-permute-start(bf16[2064,128]{1,0:T(8,128)(2,1)S(1)} %get-tuple-element.30.refs_1_), channel_id=1, source_target_pairs={{0,16},{2,18},{4,20},{6,22},{8,24},{10,26},{12,28},{14,30},{16,32}... | collective-permute-start | bytes 1585160 | tf_op jit(solution)/shard_map/ppermute | solution.py:272
  33.0 3.8 %own_b.1.refs_9_ = f32[16,128]{1,0:T(8,128)S(1)} custom-call(bf16[2064,128]{1,0:T(8,128)(2,1)S(1)} %get-tuple-element.27.refs_0_.refs_3_, bf16[2064,128]{1,0:T(8,128)(2,1)S(1)} %get-tuple-element.30.refs_1_, s32[16,128]{1,0:T(8,128)S(1)} %bitcast.5), custom_call_target="tpu_custom_call" | custom-call | flops 1073741824 | bytes 1048576 | tf_op jit(solution)/shard_map/own_b/pallas_call | solution.py:212
  36.9 2.8 %middle_a.1.refs_3_.refs_11_ = f32[16,128]{1,0:T(8,128)S(1)} custom-call(bf16[2064,128]{1,0:T(8,128)(2,1)S(1)} %collective-permute-done.5.refs_0_, bf16[2064,128]{1,0:T(8,128)(2,1)S(1)} %get-tuple-element.21.refs_1_), custom_call_target="tpu_custom_call" | custom-call | flops 1073741824 | bytes 1048576 | tf_op jit(solution)/shard_map/middle_a/pallas_call | solution.py:212
  39.7 2.7 %last_a.1.refs_2_ = f32[16,128]{1,0:T(8,128)S(1)} custom-call(bf16[2064,128]{1,0:T(8,128)(2,1)S(1)} %collective-permute-done.5.refs_0_, bf16[2064,128]{1,0:T(8,128)(2,1)S(1)} %collective-permute-done.6.refs_1_, bf16[2064,128]{1,0:T(8,128)(2,1)S(1)} %collective-permute-done.3.refs_2_.refs_5_, bf16[2064,128]{1,0:T(8,128)(2,1)S(1)} %collective-permute-done.7.refs_3_.refs_6_), custom_call_target="tpu_custom_call" | custom-call | flops 1073741824 | bytes 1048576 | tf_op jit(solution)/shard_map/last_a/pallas_call | solution.py:212
  42.4 2.9 %middle_b.1.refs_4_.refs_12_ = f32[16,128]{1,0:T(8,128)S(1)} custom-call(bf16[2064,128]{1,0:T(8,128)(2,1)S(1)} %collective-permute-done.2.refs_0_.refs_4_, bf16[2064,128]{1,0:T(8,128)(2,1)S(1)} %get-tuple-element.30.refs_1_, bf16[2064,128]{1,0:T(8,128)(2,1)S(1)} %collective-permute-done.refs_2_.refs_0_), custom_call_target="tpu_custom_call" | custom-call | flops 2147483648 | bytes 2097152 | tf_op jit(solution)/shard_map/middle_b/pallas_call | solution.py:212
  45.3 0.6 collective-permute-done.4.refs_1_.refs_2_
  45.9 2.9 %last_b.1 = f32[16,128]{1,0:T(8,128)S(1)} custom-call(bf16[2064,128]{1,0:T(8,128)(2,1)S(1)} %collective-permute-done.2.refs_0_.refs_4_, bf16[2064,128]{1,0:T(8,128)(2,1)S(1)} %collective-permute-done.4.refs_1_.refs_2_, f32[16,128]{1,0:T(8,128)S(1)} %last_a.1.refs_2_, f32[16,128]{1,0:T(8,128)S(1)} %middle_a.1.refs_3_.refs_11_, ...), custom_call_target="tpu_custom_call" | custom-call | flops 1073741824 | bytes 1048576 | tf_op jit(solution)/shard_map/last_b/pallas_call | solution.py:212
  48.8 2.7 %collective-permute-start.8 = (f32[16,128]{1,0:T(8,128)S(1)}, f32[16,128]{1,0:T(8,128)S(1)}, u32[]{:S(2)}, u32[]{:S(2)}) collective-permute-start(f32[16,128]{1,0:T(8,128)S(1)} %last_b.1), channel_id=1, source_target_pairs={{16,0},{18,2},{20,4},{22,6},{24,8},{26,10},{28,12},{30,14},{32,16}... | collective-permute-start | bytes 24584 | tf_op jit(solution)/shard_map/ppermute | solution.py:272
  51.5 5.3 %near.1 = f32[16,128]{1,0:T(8,128)S(1)} custom-call(bf16[2064,128]{1,0:T(8,128)(2,1)S(1)} %collective-permute-done.refs_2_.refs_0_, bf16[2064,128]{1,0:T(8,128)(2,1)S(1)} %get-tuple-element.30.refs_1_, bf16[2064,128]{1,0:T(8,128)(2,1)S(1)} %collective-permute-done.4.refs_1_.refs_2_, bf16[2064,128]{1,0:T(8,128)(2,1)S(1)} %get-tuple-element.27.refs_0_.refs_3_, ...), custom_call_target="tpu_custom_call" | custom-call | flops 3221225472 | bytes 3145728 | tf_op jit(solution)/shard_map/near/pallas_call | solution.py:212
  56.8 13.6 %all_to_all.9 = f32[16,1,128]{2,1,0:T(1,128)S(1)} all-to-all(f32[16,1,128]{2,1,0:T(1,128)S(1)} %bitcast.6), channel_id=1, replica_groups=mesh['ctx'=16,'head'=16] {'head'}, dimensions={0} | all-to-all | bytes 16384 | tf_op jit(solution)/shard_map/all_to_all | solution.py:355
  70.5 0.5 reduce_sum.9
  (8 shorter events, 0.0 us)
Async XLA Ops:
  0.0 11.4 %copy-start = (s32[2048]{0:T(1024)S(1)}, s32[2048]{0:T(1024)}, u32[]{:S(2)}) copy-start(s32[2048]{0:T(1024)} %param.7) | copy-start | bytes 24580
  1.6 13.9 %collective-permute-start.1 = (bf16[2064,128]{1,0:T(8,128)(2,1)S(1)}, bf16[2064,128]{1,0:T(8,128)(2,1)S(1)}, u32[]{:S(2)}, u32[]{:S(2)}) collective-permute-start(bf16[2064,128]{1,0:T(8,128)(2,1)S(1)} %get-tuple-element.20.refs_0_.refs_7_), channel_id=1, source_target_pairs={{1,17},{3,19},{5,21},{7,23},{9,25},{11,27},{13,29},{15,31},{16,0},... | collective-permute-start | bytes 1585160 | tf_op jit(solution)/shard_map/ppermute | solution.py:272
  5.2 16.0 %collective-permute-start = (bf16[2064,128]{1,0:T(8,128)(2,1)S(1)}, bf16[2064,128]{1,0:T(8,128)(2,1)S(1)}, u32[]{:S(2)}, u32[]{:S(2)}) collective-permute-start(bf16[2064,128]{1,0:T(8,128)(2,1)S(1)} %get-tuple-element.27.refs_0_.refs_3_), channel_id=1, source_target_pairs={{1,17},{3,19},{5,21},{7,23},{9,25},{11,27},{13,29},{15,31},{16,0},... | collective-permute-start | bytes 1585160 | tf_op jit(solution)/shard_map/ppermute | solution.py:272
  8.7 14.7 %collective-permute-start.3 = (bf16[2064,128]{1,0:T(8,128)(2,1)S(1)}, bf16[2064,128]{1,0:T(8,128)(2,1)S(1)}, u32[]{:S(2)}, u32[]{:S(2)}) collective-permute-start(bf16[2064,128]{1,0:T(8,128)(2,1)S(1)} %get-tuple-element.21.refs_1_), channel_id=1, source_target_pairs={{17,1},{19,3},{21,5},{23,7},{25,9},{27,11},{29,13},{31,15},{33,17}... | collective-permute-start | bytes 1585160 | tf_op jit(solution)/shard_map/ppermute | solution.py:284
  10.7 22.3 %collective-permute-start.6 = (bf16[2064,128]{1,0:T(8,128)(2,1)S(1)}, bf16[2064,128]{1,0:T(8,128)(2,1)S(1)}, u32[]{:S(2)}, u32[]{:S(2)}) collective-permute-start(bf16[2064,128]{1,0:T(8,128)(2,1)S(1)} %get-tuple-element.21.refs_1_), channel_id=1, source_target_pairs={{0,16},{2,18},{4,20},{6,22},{8,24},{10,26},{12,28},{14,30},{16,32}... | collective-permute-start | bytes 1585160 | tf_op jit(solution)/shard_map/ppermute | solution.py:272
  15.5 21.4 %collective-permute-start.5 = (bf16[2064,128]{1,0:T(8,128)(2,1)S(1)}, bf16[2064,128]{1,0:T(8,128)(2,1)S(1)}, u32[]{:S(2)}, u32[]{:S(2)}) collective-permute-start(bf16[2064,128]{1,0:T(8,128)(2,1)S(1)} %collective-permute-done.1.refs_0_), channel_id=1, source_target_pairs={{1,17},{3,19},{5,21},{7,23},{9,25},{11,27},{13,29},{15,31},{16,0},... | collective-permute-start | bytes 1585160 | tf_op jit(solution)/shard_map/ppermute | solution.py:272
  23.4 16.3 %collective-permute-start.7 = (bf16[2064,128]{1,0:T(8,128)(2,1)S(1)}, bf16[2064,128]{1,0:T(8,128)(2,1)S(1)}, u32[]{:S(2)}, u32[]{:S(2)}) collective-permute-start(bf16[2064,128]{1,0:T(8,128)(2,1)S(1)} %collective-permute-done.3.refs_2_.refs_5_), channel_id=1, source_target_pairs={{0,113},{2,115},{4,117},{6,119},{8,121},{10,123},{12,125},{14,127}} | collective-permute-start | bytes 1585160 | tf_op jit(solution)/shard_map/ppermute | solution.py:291
  24.1 18.3 %collective-permute-start.2 = (bf16[2064,128]{1,0:T(8,128)(2,1)S(1)}, bf16[2064,128]{1,0:T(8,128)(2,1)S(1)}, u32[]{:S(2)}, u32[]{:S(2)}) collective-permute-start(bf16[2064,128]{1,0:T(8,128)(2,1)S(1)} %collective-permute-done.refs_2_.refs_0_), channel_id=1, source_target_pairs={{1,17},{3,19},{5,21},{7,23},{9,25},{11,27},{13,29},{15,31},{16,0},... | collective-permute-start | bytes 1585160 | tf_op jit(solution)/shard_map/ppermute | solution.py:272
  29.5 16.4 %collective-permute-start.4 = (bf16[2064,128]{1,0:T(8,128)(2,1)S(1)}, bf16[2064,128]{1,0:T(8,128)(2,1)S(1)}, u32[]{:S(2)}, u32[]{:S(2)}) collective-permute-start(bf16[2064,128]{1,0:T(8,128)(2,1)S(1)} %get-tuple-element.30.refs_1_), channel_id=1, source_target_pairs={{0,16},{2,18},{4,20},{6,22},{8,24},{10,26},{12,28},{14,30},{16,32}... | collective-permute-start | bytes 1585160 | tf_op jit(solution)/shard_map/ppermute | solution.py:272
  48.8 8.0 %collective-permute-start.8 = (f32[16,128]{1,0:T(8,128)S(1)}, f32[16,128]{1,0:T(8,128)S(1)}, u32[]{:S(2)}, u32[]{:S(2)}) collective-permute-start(f32[16,128]{1,0:T(8,128)S(1)} %last_b.1), channel_id=1, source_target_pairs={{16,0},{18,2},{20,4},{22,6},{24,8},{26,10},{28,12},{30,14},{32,16}... | collective-permute-start | bytes 24584 | tf_op jit(solution)/shard_map/ppermute | solution.py:272
